TPU v7x, 128 devices: a whole 4x4x4 slice. The times are simulated.
128 devices in a mesh: dom: 128 (over z, x, y, core).
Axes of the slice: x: 4, y: 4, z: 4, core: 2. Of those that a mesh axis runs over, the one named last changes fastest.
Arguments:
- node_latent: bfloat16 [65536, 512], P('dom'), may hold values from -6 to 6
- edge_latent: bfloat16 [262144, 512], P('dom'), may hold values from -6 to 6
- sender_index: int32 [262144], P('dom'), may hold values from 0 to 1535, as said below
- receiver_index: int32 [262144], P('dom'), may hold values from 0 to 511
- send_rows: int32 [128, 128, 8], P('dom'), may hold values from 0 to 511
- node_count: int32 [128], P('dom'), may hold values from 256 to 512, as said below
- edge_proj_in: bfloat16 [1, 1536, 512], replicated, may hold values from -0.15625 to 0.15625
- edge_bias_in: float32 [1, 512], replicated, may hold values from -3 to 3
- edge_proj_out: bfloat16 [1, 512, 512], replicated, may hold values from -0.25 to 0.25
- edge_bias_out: float32 [1, 512], replicated, may hold values from -3 to 3
- edge_gain: float32 [1, 512], replicated, may hold values from 0.1 to 1.9
- node_proj_in: bfloat16 [1, 1024, 512], replicated, may hold values from -0.1875 to 0.1875
- node_bias_in: float32 [1, 512], replicated, may hold values from -3 to 3
- node_proj_out: bfloat16 [1, 512, 512], replicated, may hold values from -0.25 to 0.25
- node_bias_out: float32 [1, 512], replicated, may hold values from -3 to 3
- node_gain: float32 [1, 512], replicated, may hold values from 0.1 to 1.9
- node_cot: float32 [65536, 512], P('dom'), may hold values from -6 to 6
- edge_cot: float32 [262144, 512], P('dom'), may hold values from -6 to 6
Outputs:
- node_out: bfloat16 [65536, 512], P('dom')
- edge_out: bfloat16 [262144, 512], P('dom')
- node_grad: float32 [65536, 512], P('dom')
- edge_grad: float32 [262144, 512], P('dom')
- edge_in_grad: float32 [1, 1536, 512], P(None, 'dom')
- edge_out_grad: float32 [1, 512, 512], P(None, 'dom')
- node_in_grad: float32 [1, 1024, 512], P(None, 'dom')
- node_out_grad: float32 [1, 512, 512], P(None, 'dom')
Inputs may be any that keep to these rules, and one draw needn't show every extreme that they name: `sender_index`: values below 512 name a node of the edge's own partition; 512 + p * 8 + k names entry k of the list that partition p sends to the edge's partition d. Most senders are local; remote ones come from partitions p = (d + t) mod 128 with t in -4 .. 4 or t = 64, never p = d. `receiver_index`: local node numbers of the edge's own partition; receivers at or above the partition's node count are padding. send_rows[p, q] lists local nodes of partition p; entries may repeat. `node_count`: some partition holds exactly 512 real nodes and some exactly 256.
All inputs are finite; a program needn't handle non-finite values.
Results may differ from a plain program's by a relative error of at most 0.017.
Values may be sent and summed in bfloat16 or wider, within the bound.
A program may use at most 192 MiB of HBM per device.

v0:
```python
import functools

import jax
import jax.numpy as jnp
from jax import lax
from jax.experimental import pallas as pl
from jax.experimental.pallas import tpu as pltpu
from jax.sharding import PartitionSpec as P

EPS = 1e-05
MESH = pl.DeviceIdType.MESH
BF = jnp.bfloat16
F32 = jnp.float32
I32 = jnp.int32

L = 512
N = 512
E = 2048
HB = 8
SLOTS = 9
HALO = SLOTS * HB
HPAD = 128
TAB = N + HPAD
C = 256
CHUNKS = E // C
XW = L + TAB + N
VMEM_LIMIT = 56 * 1024 * 1024

NT = (((1,), (1,)), ((), ()))
TN = (((0,), (0,)), ((), ()))


def slot_shift(slot):
    return 64 if slot == 4 else slot - 4


def mm(a, b):
    return jnp.dot(a, b, preferred_element_type=F32)


def mm_nt(a, b):
    return lax.dot_general(a, b, NT, preferred_element_type=F32)


def mm_tn(a, b):
    return lax.dot_general(a, b, TN, preferred_element_type=F32)


def sigmoid(x):
    return 0.5 * jnp.tanh(0.5 * x) + 0.5


def table_index(sender, me, n_dom):
    far = sender - N
    peer = far // HB
    row = far - peer * HB
    turn = lax.rem(peer - me + (n_dom + 4), n_dom)
    slot = jnp.where(turn == 68, 4, turn)
    return jnp.where(sender < N, sender, N + slot * HB + row)


def greet(devices):
    barrier = pltpu.get_barrier_semaphore()
    for device in devices:
        pl.semaphore_signal(barrier, inc=1, device_id=(device,), device_id_type=MESH)
    pl.semaphore_wait(barrier, len(devices))


def halo_kernel(n_dom, h_ref, rows_ref, out_ref, wide, outgoing, incoming, send_sem, recv_sem):
    me = lax.axis_index("dom")
    targets = [lax.rem(me - slot_shift(s) + n_dom, n_dom) for s in range(SLOTS)]
    wide[...] = h_ref[...].astype(F32)
    barrier = pltpu.get_barrier_semaphore()
    for device in targets:
        pl.semaphore_signal(barrier, inc=1, device_id=(device,), device_id_type=MESH)
    for s in range(SLOTS):
        for k in range(HB):
            row = rows_ref[targets[s] * HB + k]
            outgoing[pl.ds(s * HB + k, 1), :] = wide[pl.ds(row, 1), :]
    pl.semaphore_wait(barrier, SLOTS)
    copies = []
    for s in range(SLOTS):
        copy = pltpu.make_async_remote_copy(
            src_ref=outgoing.at[pl.ds(s * HB, HB)],
            dst_ref=incoming.at[pl.ds(s * HB, HB)],
            send_sem=send_sem.at[s],
            recv_sem=recv_sem.at[s],
            device_id=(targets[s],),
            device_id_type=MESH,
        )
        copy.start()
        copies.append(copy)
    for copy in copies:
        copy.wait()
    out_ref[...] = jnp.concatenate(
        [incoming[...].astype(BF), jnp.zeros((HPAD - HALO, L), BF)], axis=0
    )


def fetch_halo(node_rows, slot_rows, n_dom):
    return pl.pallas_call(
        functools.partial(halo_kernel, n_dom),
        out_shape=jax.ShapeDtypeStruct((HPAD, L), BF),
        in_specs=[
            pl.BlockSpec(memory_space=pltpu.VMEM),
            pl.BlockSpec(memory_space=pltpu.SMEM),
        ],
        out_specs=pl.BlockSpec(memory_space=pltpu.VMEM),
        scratch_shapes=[
            pltpu.VMEM((N, L), F32),
            pltpu.VMEM((HALO, L), F32),
            pltpu.VMEM((HALO, L), F32),
            pltpu.SemaphoreType.DMA((SLOTS,)),
            pltpu.SemaphoreType.DMA((SLOTS,)),
        ],
        compiler_params=pltpu.CompilerParams(collective_id=0, has_side_effects=True),
        name="halo",
    )(node_rows, slot_rows)


def norm_forward(raw):
    centered = raw - jnp.mean(raw, axis=-1, keepdims=True)
    inv = lax.rsqrt(jnp.mean(centered * centered, axis=-1, keepdims=True) + EPS)
    return centered * inv, inv


def norm_backward(q, normed, inv):
    first = jnp.mean(q, axis=-1, keepdims=True)
    second = jnp.mean(q * normed, axis=-1, keepdims=True)
    return inv * (q - first - normed * second)


def act_slope(pre):
    gate = sigmoid(pre)
    return gate * (1.0 + pre * (1.0 - gate))


def rows_kernel(
    n_dom,
    snd_ref, rcv_ref, cnt_ref, h_hbm, halo_hbm, e_hbm, pin_hbm, b_in, pout_hbm, b_out, gain,
    npin_hbm, nb_in, npout_hbm, nb_out, ngain, ncot_hbm, ecot_hbm,
    nout_hbm, eout_hbm, egrad_hbm, dpre_hbm, draw_hbm, hid_hbm, gnode_hbm, npart_hbm,
    idx_v, x_v, rt_v, w_v, tab_v, pin_v, pout_v, npin_v, npout_v, ncot_v, cot_v,
    pre_v, hid_v, n_v, inv_v, enew_v, draw_v, dpre_v, nx_v, dy_v, nout_v, npart_v, gnode_v,
    in_sem, e_sem, cot_sem, eout_sem, hid_sem, draw_sem, dpre_sem, egrad_sem, out_sem,
):
    me = lax.axis_index("dom")

    def load(k, src, dst):
        return pltpu.make_async_copy(src, dst, in_sem.at[k])

    def rows(i):
        return pl.ds(pl.multiple_of(i * C, C), C)

    def e_load(i):
        return pltpu.make_async_copy(e_hbm.at[rows(i)], x_v.at[rows(i), pl.ds(0, L)], e_sem.at[i])

    def cot_load(i):
        return pltpu.make_async_copy(ecot_hbm.at[rows(i)], cot_v.at[rows(i)], cot_sem.at[i])

    def put(i, src, dst, sem):
        return pltpu.make_async_copy(src.at[rows(i)], dst.at[rows(i)], sem.at[i])

    loads = [
        load(0, h_hbm, tab_v.at[pl.ds(0, N)]),
        load(1, halo_hbm, tab_v.at[pl.ds(N, HPAD)]),
        load(2, pin_hbm, pin_v),
        load(3, pout_hbm, pout_v),
        load(4, npin_hbm, npin_v),
        load(5, npout_hbm, npout_v),
        load(6, ncot_hbm, ncot_v),
    ]
    for k in range(3):
        loads[k].start()
    for i in range(CHUNKS):
        e_load(i).start()
    for k in range(3, 7):
        loads[k].start()
    for i in range(CHUNKS):
        cot_load(i).start()

    idx_v[...] = table_index(snd_ref[...], me, n_dom)
    lane = lax.broadcasted_iota(I32, (128, 128), 1)
    high = lax.broadcasted_iota(I32, (N, 128), 0)

    for k in range(3):
        loads[k].wait()
    w_v[0:L, :] = pin_v[0:L, :]
    w_v[L : L + TAB, :] = mm(tab_v[...], pin_v[L : 2 * L, :]).astype(BF)
    w_v[L + TAB :, :] = (mm(tab_v[0:N, :], pin_v[2 * L :, :]) + b_in[...]).astype(BF)
    loads[3].wait()

    def forward(i, carry):
        e_load(i).wait()
        for b in range(C // 128):
            block = i * (C // 128) + b
            at = pl.ds(pl.multiple_of(block * 128, 128), 128)
            s_col = jnp.broadcast_to(idx_v[pl.ds(block, 1), :], (128, 128)).T
            r_row = rcv_ref[pl.ds(block, 1), :]
            r_col = jnp.broadcast_to(r_row, (128, 128)).T
            for m in range(TAB // 128):
                x_v[at, L + 128 * m : L + 128 * (m + 1)] = (s_col == lane + 128 * m).astype(F32).astype(BF)
            for m in range(N // 128):
                x_v[at, L + TAB + 128 * m : L + TAB + 128 * (m + 1)] = (
                    (r_col == lane + 128 * m).astype(F32).astype(BF)
                )
            rt_v[:, at] = (jnp.broadcast_to(r_row, (N, 128)) == high).astype(F32).astype(BF)
        pre = mm(x_v[rows(i), :], w_v[...])
        pre_v[rows(i), :] = pre
        hid = (pre * sigmoid(pre)).astype(BF)
        hid_v[rows(i), :] = hid
        raw = mm(hid, pout_v[...]) + b_out[...]
        normed, inv = norm_forward(raw)
        n_v[rows(i), :] = normed
        inv_v[rows(i), :] = inv
        enew_v[rows(i), :] = (x_v[rows(i), 0:L].astype(F32) + normed * gain[...]).astype(BF)
        put(i, enew_v, eout_hbm, eout_sem).start()
        put(i, hid_v, hid_hbm, hid_sem).start()
        return carry

    lax.fori_loop(0, CHUNKS, forward, 0)

    valid = (lax.broadcasted_iota(I32, (N, 1), 0) < cnt_ref[0]).astype(F32)
    nx_v[:, 0:L] = tab_v[0:N, :]
    nx_v[:, L:] = (mm(rt_v[...], enew_v[...]) * valid).astype(BF)
    for k in range(4, 7):
        loads[k].wait()
    pre = mm(nx_v[...], npin_v[...]) + nb_in[...]
    hid = (pre * sigmoid(pre)).astype(BF)
    normed, inv = norm_forward(mm(hid, npout_v[...]) + nb_out[...])
    nout_v[...] = (tab_v[0:N, :].astype(F32) + valid * (normed * ngain[...])).astype(BF)
    nout_copy = pltpu.make_async_copy(nout_v, nout_hbm, out_sem.at[0])
    nout_copy.start()
    draw = norm_backward(valid * ncot_v[...] * ngain[...], normed, inv).astype(BF)
    dpre = (mm_nt(draw, npout_v[...]) * act_slope(pre)).astype(BF)
    npart_v[...] = ncot_v[...] + mm_nt(dpre, npin_v[0:L, :])
    npart_copy = pltpu.make_async_copy(npart_v, npart_hbm, out_sem.at[1])
    npart_copy.start()
    dy_v[...] = mm_nt(dpre, npin_v[L:, :]).astype(BF)
    gnode_v[:, 0:64, :] = mm_tn(nx_v[...], dpre).astype(BF).reshape(16, 64, L)
    gnode_v[:, 64:96, :] = mm_tn(hid, draw).astype(BF).reshape(16, 32, L)
    gnode_copy = pltpu.make_async_copy(gnode_v, gnode_hbm, out_sem.at[2])
    gnode_copy.start()

    def backward(i, carry):
        cot_load(i).wait()
        total = cot_v[rows(i), :] + mm(x_v[rows(i), L + TAB :], dy_v[...])
        draw = norm_backward(total * gain[...], n_v[rows(i), :], inv_v[rows(i), :]).astype(BF)
        draw_v[rows(i), :] = draw
        put(i, draw_v, draw_hbm, draw_sem).start()
        dpre = (mm_nt(draw, pout_v[...]) * act_slope(pre_v[rows(i), :])).astype(BF)
        dpre_v[rows(i), :] = dpre
        put(i, dpre_v, dpre_hbm, dpre_sem).start()
        cot_v[rows(i), :] = total + mm_nt(dpre, pin_v[0:L, :])
        put(i, cot_v, egrad_hbm, egrad_sem).start()
        return carry

    lax.fori_loop(0, CHUNKS, backward, 0)
    nout_copy.wait()
    npart_copy.wait()
    gnode_copy.wait()
    for i in range(CHUNKS):
        put(i, enew_v, eout_hbm, eout_sem).wait()
        put(i, hid_v, hid_hbm, hid_sem).wait()
        put(i, draw_v, draw_hbm, draw_sem).wait()
        put(i, dpre_v, dpre_hbm, dpre_sem).wait()
        put(i, cot_v, egrad_hbm, egrad_sem).wait()


def run_rows(n_dom, *operands):
    hbm = pl.BlockSpec(memory_space=pl.ANY)
    vmem = pl.BlockSpec(memory_space=pltpu.VMEM)
    smem = pl.BlockSpec(memory_space=pltpu.SMEM)
    shape = jax.ShapeDtypeStruct
    dma = pltpu.SemaphoreType.DMA
    return pl.pallas_call(
        functools.partial(rows_kernel, n_dom),
        out_shape=[
            shape((N, L), BF),
            shape((E, L), BF),
            shape((E, L), F32),
            shape((E, L), BF),
            shape((E, L), BF),
            shape((E, L), BF),
            shape((16, 96, L), BF),
            shape((N, L), F32),
        ],
        in_specs=[vmem, vmem, smem, hbm, hbm, hbm, hbm, vmem, hbm, vmem, vmem]
        + [hbm, vmem, hbm, vmem, vmem, hbm, hbm],
        out_specs=[hbm] * 8,
        scratch_shapes=[
            pltpu.VMEM((16, 128), I32),
            pltpu.VMEM((E, XW), BF),
            pltpu.VMEM((N, E), BF),
            pltpu.VMEM((XW, L), BF),
            pltpu.VMEM((TAB, L), BF),
            pltpu.VMEM((3 * L, L), BF),
            pltpu.VMEM((L, L), BF),
            pltpu.VMEM((2 * L, L), BF),
            pltpu.VMEM((L, L), BF),
            pltpu.VMEM((N, L), F32),
            pltpu.VMEM((E, L), F32),
            pltpu.VMEM((E, L), F32),
            pltpu.VMEM((E, L), BF),
            pltpu.VMEM((E, L), F32),
            pltpu.VMEM((E, 1), F32),
            pltpu.VMEM((E, L), BF),
            pltpu.VMEM((E, L), BF),
            pltpu.VMEM((E, L), BF),
            pltpu.VMEM((N, 2 * L), BF),
            pltpu.VMEM((N, L), BF),
            pltpu.VMEM((N, L), BF),
            pltpu.VMEM((N, L), F32),
            pltpu.VMEM((16, 96, L), BF),
            dma((7,)),
            dma((CHUNKS,)),
            dma((CHUNKS,)),
            dma((CHUNKS,)),
            dma((CHUNKS,)),
            dma((CHUNKS,)),
            dma((CHUNKS,)),
            dma((CHUNKS,)),
            dma((3,)),
        ],
        compiler_params=pltpu.CompilerParams(vmem_limit_bytes=VMEM_LIMIT),
        name="rows",
    )(*operands)


WIDE = L // 2
LANES = 128


class Wave:
    def __init__(self, coords, refs):
        self.coords = coords
        (self.own, self.from_core, self.a1, self.b1, self.sa, self.sb, self.a2, self.b2) = refs[:8]
        self.send, self.recv = refs[8:]
        self.copies = []

    def start(self, src, dst, k, device):
        copy = pltpu.make_async_remote_copy(
            src_ref=src,
            dst_ref=dst,
            send_sem=self.send.at[k],
            recv_sem=self.recv.at[k],
            device_id=(device,),
            device_id_type=MESH,
        )
        copy.start()
        self.copies.append(copy)

    def to_core(self, src):
        z, x, y, c = self.coords
        self.start(src, self.from_core, 0, device_at(z, x, y, 1 - c))

    def first(self):
        z, x, y, c = self.coords
        self.copies[0].wait_recv()
        own, got = self.own, self.from_core
        for zz in range(4):
            own[zz] = (own[zz].astype(F32) + got[zz].astype(F32)).astype(BF)
        for o in range(1, 4):
            zp, xp = lax.rem(z + 4 - o, 4), lax.rem(x + 4 - o, 4)
            self.start(own.at[zp, :, :, pl.ds(0, LANES)], self.a1.at[o - 1], o, device_at(zp, x, y, c))
            self.start(own.at[:, xp, :, pl.ds(LANES, LANES)], self.b1.at[o - 1], 3 + o, device_at(z, xp, y, c))

    def second(self):
        z, x, y, c = self.coords
        for copy in self.copies[1:7]:
            copy.wait_recv()
        a = self.own[z, :, :, 0:LANES].astype(F32)
        b = self.own[:, x, :, LANES:WIDE].astype(F32)
        for o in range(3):
            a = a + self.a1[o].astype(F32)
            b = b + self.b1[o].astype(F32)
        self.sa[...] = a.astype(BF)
        self.sb[...] = b.astype(BF)
        for o in range(1, 4):
            zp, xp = lax.rem(z + 4 - o, 4), lax.rem(x + 4 - o, 4)
            self.start(self.sa.at[xp], self.a2.at[o - 1], 6 + o, device_at(z, xp, y, c))
            self.start(self.sb.at[zp], self.b2.at[o - 1], 9 + o, device_at(zp, x, y, c))

    def third(self, block, at):
        z, x, y, c = self.coords
        for copy in self.copies[7:13]:
            copy.wait_recv()
        a, b = self.sa[x].astype(F32), self.sb[z].astype(F32)
        for o in range(3):
            a = a + self.a2[o].astype(F32)
            b = b + self.b2[o].astype(F32)
        block[at, 0:LANES] = a.astype(BF)
        block[at, LANES:WIDE] = b.astype(BF)

    def finish(self):
        for copy in self.copies:
            copy.wait_send()


def device_at(z, x, y, c):
    return ((z * 4 + x) * 4 + y) * 2 + c


def wave_scratch(depth):
    dma = pltpu.SemaphoreType.DMA
    return [
        pltpu.VMEM((4, 4, depth, WIDE), BF),
        pltpu.VMEM((4, 4, depth, WIDE), BF),
        pltpu.VMEM((3, 4, depth, LANES), BF),
        pltpu.VMEM((3, 4, depth, LANES), BF),
        pltpu.VMEM((4, depth, LANES), BF),
        pltpu.VMEM((4, depth, LANES), BF),
        pltpu.VMEM((3, depth, LANES), BF),
        pltpu.VMEM((3, depth, LANES), BF),
        dma((13,)),
        dma((13,)),
    ]


def sums_kernel(
    n_dom,
    snd_ref, rcv_ref, gnode_hbm, h_hbm, halo_hbm, e_hbm, pin_hbm, hid_hbm, draw_hbm, dpre_hbm,
    out_ref, part_ref, ret_ref,
    tab_v, e_v, hid_v, draw_v, dpre_v, ps_v, pr_v, st_v, rt_v, as_v, ar_v, there_in, there_out, y_v,
    block, sorted_v, got, in_sem, y_send, y_recv, last_send, last_recv,
    *wave_refs,
):
    me = lax.axis_index("dom")
    c = lax.rem(me, 2)
    y = lax.rem(me // 2, 4)
    x = lax.rem(me // 8, 4)
    z = me // 32
    m = lax.rem(me, 8)
    coords = (z, x, y, c)
    node_wave = Wave(coords, wave_refs[0:10])
    in_wave = Wave(coords, wave_refs[10:20])
    out_wave = Wave(coords, wave_refs[20:30])

    mine = pl.ds(pl.multiple_of(c * WIDE, WIDE), WIDE)
    theirs = pl.ds(pl.multiple_of((1 - c) * WIDE, WIDE), WIDE)
    halves = (theirs, mine)

    loads = []

    def load(src, dst):
        copy = pltpu.make_async_copy(src, dst, in_sem.at[len(loads)])
        copy.start()
        loads.append(copy)

    load(dpre_hbm.at[:, theirs], dpre_v.at[0])
    load(h_hbm, tab_v.at[pl.ds(0, N)])
    load(halo_hbm, tab_v.at[pl.ds(N, HPAD)])
    load(e_hbm, e_v)
    load(dpre_hbm.at[:, mine], dpre_v.at[1])
    for k in range(4):
        load(gnode_hbm.at[pl.ds(4 * k, 4), :, mine], node_wave.own.at[k])
    load(hid_hbm, hid_v)
    load(draw_hbm.at[:, theirs], draw_v.at[0])
    load(draw_hbm.at[:, mine], draw_v.at[1])
    for half in range(2):
        load(pin_hbm.at[pl.ds(L, L), halves[half]], ps_v.at[half])
        load(pin_hbm.at[pl.ds(2 * L, L), halves[half]], pr_v.at[half])

    owners = [lax.rem(me + slot_shift(s) + n_dom, n_dom) for s in range(SLOTS)]
    others = [device_at(z, x, 0, 0) + lax.rem(m + 8 - o, 8) for o in range(1, 8)]
    along = [device_at(lax.rem(z + o, 4), x, y, c) for o in range(1, 4)]
    along += [device_at(z, lax.rem(x + o, 4), y, c) for o in range(1, 4)]
    greet(owners + others + along)

    node_wave.start(
        gnode_hbm.at[:, :, theirs],
        node_wave.from_core.reshape(16, 96, WIDE),
        0,
        device_at(z, x, y, 1 - c),
    )

    index = table_index(snd_ref[...], me, n_dom)
    high = lax.broadcasted_iota(I32, (TAB, 128), 0)
    for k in range(E // 128):
        at = pl.ds(k * 128, 128)
        st_v[:, at] = (jnp.broadcast_to(index[k : k + 1, :], (TAB, 128)) == high).astype(F32).astype(BF)
        rt_v[:, at] = (
            (jnp.broadcast_to(rcv_ref[k : k + 1, :], (N, 128)) == high[0:N, :]).astype(F32).astype(BF)
        )

    for k in range(4):
        loads[k].wait()

    def in_products(half, dst):
        dpre = dpre_v[half]
        sent = mm(st_v[...], dpre).astype(BF)
        taken = mm(rt_v[...], dpre).astype(BF)
        as_v[half] = sent
        ar_v[half] = taken
        product = jnp.concatenate(
            [mm_tn(e_v[...], dpre), mm_tn(tab_v[...], sent), mm_tn(tab_v[0:N, :], taken)], axis=0
        )
        dst[...] = product.astype(BF).reshape(4, 4, 96, WIDE)

    def out_products(half, dst):
        dst[...] = mm_tn(hid_v[...], draw_v[half]).astype(BF).reshape(4, 4, 32, WIDE)

    in_products(0, there_in)
    in_wave.to_core(there_in)
    for k in range(5, 9):
        loads[k].wait()
    node_wave.first()
    loads[4].wait()
    in_products(1, in_wave.own)
    in_wave.first()
    node_wave.second()

    for k in range(9, 16):
        loads[k].wait()
    out_products(0, there_out)
    out_wave.to_core(there_out)
    out_products(1, out_wave.own)

    y_v[...] = mm_nt(as_v[0, N : N + HALO, :], ps_v[0]) + mm_nt(as_v[1, N : N + HALO, :], ps_v[1])
    returns = []
    for s in range(SLOTS):
        copy = pltpu.make_async_remote_copy(
            src_ref=y_v.at[pl.ds(s * HB, HB)],
            dst_ref=ret_ref.at[pl.ds(s * HB, HB)],
            send_sem=y_send.at[s],
            recv_sem=y_recv.at[s],
            device_id=(owners[s],),
            device_id_type=MESH,
        )
        copy.start()
        returns.append(copy)
    out_wave.first()
    part_ref[...] = (
        mm_nt(as_v[0, 0:N, :], ps_v[0])
        + mm_nt(as_v[1, 0:N, :], ps_v[1])
        + mm_nt(ar_v[0], pr_v[0])
        + mm_nt(ar_v[1], pr_v[1])
    ).astype(BF)
    node_wave.third(block, pl.ds(0, 96))
    in_wave.second()
    out_wave.second()
    in_wave.third(block, pl.ds(96, 96))
    out_wave.third(block, pl.ds(192, 32))

    row = lax.broadcasted_iota(I32, (256, 224), 0)
    col = lax.broadcasted_iota(I32, (256, 224), 1)
    j = row // 32
    r = row - j * 32
    source = jnp.where(
        r < 8,
        8 * j + r,
        jnp.where(
            r < 12,
            64 + 4 * j + (r - 8),
            jnp.where(r < 24, 96 + 12 * j + (r - 12), jnp.where(r < 28, 192 + 4 * j + (r - 24), -1)),
        ),
    )
    order = (source == col).astype(F32).astype(BF)
    sorted_v[...] = mm(order, block[...]).astype(BF).reshape(8, 32, WIDE)
    lasts = []
    for o in range(1, 8):
        target = lax.rem(m + 8 - o, 8)
        copy = pltpu.make_async_remote_copy(
            src_ref=sorted_v.at[target],
            dst_ref=got.at[o - 1],
            send_sem=last_send.at[o - 1],
            recv_sem=last_recv.at[o - 1],
            device_id=(others[o - 1],),
            device_id_type=MESH,
        )
        copy.start()
        lasts.append(copy)
    for copy in lasts:
        copy.wait_recv()
    same = sorted_v[m].astype(F32)
    for o in (2, 4, 6):
        same = same + got[o - 1].astype(F32)
    cross = got[0].astype(F32)
    for o in (3, 5, 7):
        cross = cross + got[o - 1].astype(F32)
    even = c == 0
    out_ref[:, 0:WIDE] = jnp.where(even, same, cross)
    out_ref[:, WIDE:] = jnp.where(even, cross, same)
    for copy in returns:
        copy.wait()
    for copy in lasts:
        copy.wait_send()
    for wave in (node_wave, in_wave, out_wave):
        wave.finish()


def run_sums(n_dom, *operands):
    hbm = pl.BlockSpec(memory_space=pl.ANY)
    vmem = pl.BlockSpec(memory_space=pltpu.VMEM)
    shape = jax.ShapeDtypeStruct
    dma = pltpu.SemaphoreType.DMA
    return pl.pallas_call(
        functools.partial(sums_kernel, n_dom),
        out_shape=[shape((32, L), F32), shape((N, L), BF), shape((HALO, L), F32)],
        in_specs=[vmem, vmem] + [hbm] * 8,
        out_specs=[vmem, vmem, vmem],
        scratch_shapes=[
            pltpu.VMEM((TAB, L), BF),
            pltpu.VMEM((E, L), BF),
            pltpu.VMEM((E, L), BF),
            pltpu.VMEM((2, E, WIDE), BF),
            pltpu.VMEM((2, E, WIDE), BF),
            pltpu.VMEM((2, L, WIDE), BF),
            pltpu.VMEM((2, L, WIDE), BF),
            pltpu.VMEM((TAB, E), BF),
            pltpu.VMEM((N, E), BF),
            pltpu.VMEM((2, TAB, WIDE), BF),
            pltpu.VMEM((2, N, WIDE), BF),
            pltpu.VMEM((4, 4, 96, WIDE), BF),
            pltpu.VMEM((4, 4, 32, WIDE), BF),
            pltpu.VMEM((HALO, L), F32),
            pltpu.VMEM((224, WIDE), BF),
            pltpu.VMEM((8, 32, WIDE), BF),
            pltpu.VMEM((7, 32, WIDE), BF),
            dma((16,)),
            dma((SLOTS,)),
            dma((SLOTS,)),
            dma((7,)),
            dma((7,)),
        ]
        + wave_scratch(96)
        + wave_scratch(96)
        + wave_scratch(32),
        compiler_params=pltpu.CompilerParams(
            collective_id=1, has_side_effects=True, vmem_limit_bytes=VMEM_LIMIT
        ),
        name="sums",
    )(*operands)


def last_kernel(
    n_dom, edge_factor, node_factor,
    rows_ref, sums_ref, part_ref, ret_ref, npart_ref,
    grad_ref, ein_ref, eout_ref, nin_ref, nout_ref,
):
    me = lax.axis_index("dom")
    grad_ref[...] = npart_ref[...] + part_ref[...].astype(F32)
    for s in range(SLOTS):
        reader = lax.rem(me - slot_shift(s) + n_dom, n_dom)
        for k in range(HB):
            at = pl.ds(rows_ref[reader * HB + k], 1)
            grad_ref[at, :] = grad_ref[at, :] + ret_ref[s * HB + k : s * HB + k + 1, :]
    nin_ref[0] = sums_ref[0:8, :] * node_factor
    nout_ref[0] = sums_ref[8:12, :] * node_factor
    ein_ref[0] = sums_ref[12:24, :] * edge_factor
    eout_ref[0] = sums_ref[24:28, :] * edge_factor


def run_last(n_dom, edge_factor, node_factor, *operands):
    vmem = pl.BlockSpec(memory_space=pltpu.VMEM)
    smem = pl.BlockSpec(memory_space=pltpu.SMEM)
    shape = jax.ShapeDtypeStruct
    return pl.pallas_call(
        functools.partial(last_kernel, n_dom, edge_factor, node_factor),
        out_shape=[
            shape((N, L), F32),
            shape((1, 12, L), F32),
            shape((1, 4, L), F32),
            shape((1, 8, L), F32),
            shape((1, 4, L), F32),
        ],
        in_specs=[smem, vmem, vmem, vmem, vmem],
        out_specs=[vmem] * 5,
        name="last",
    )(*operands)


def per_device(
    node_latent,
    edge_latent,
    sender_index,
    receiver_index,
    send_rows,
    node_count,
    edge_proj_in,
    edge_bias_in,
    edge_proj_out,
    edge_bias_out,
    edge_gain,
    node_proj_in,
    node_bias_in,
    node_proj_out,
    node_bias_out,
    node_gain,
    node_cot,
    edge_cot,
):
    n_dom = lax.axis_size("dom")
    slot_rows = send_rows.reshape(-1)
    snd = sender_index.reshape(E // 128, 128)
    rcv = receiver_index.reshape(E // 128, 128)
    pin, pout = edge_proj_in.reshape(3 * L, L), edge_proj_out.reshape(L, L)
    halo = fetch_halo(node_latent, slot_rows, n_dom)
    node_out, edge_out, edge_grad, dpre, draw, hid, gnode, npart = run_rows(
        n_dom, snd, rcv, node_count, node_latent, halo, edge_latent, pin, edge_bias_in, pout,
        edge_bias_out, edge_gain, node_proj_in.reshape(2 * L, L), node_bias_in,
        node_proj_out.reshape(L, L), node_bias_out, node_gain, node_cot, edge_cot,
    )
    sums, part, returned = run_sums(
        n_dom, snd, rcv, gnode, node_latent, halo, edge_latent, pin, hid, draw, dpre
    )
    edge_factor = float(E * n_dom) ** (-0.5)
    node_factor = float(N * n_dom) ** (-0.5)
    node_grad, edge_in, edge_out_grad, node_in, node_out_grad = run_last(
        n_dom, edge_factor, node_factor, slot_rows, sums, part, returned, npart
    )
    return node_out, edge_out, node_grad, edge_grad, edge_in, edge_out_grad, node_in, node_out_grad


def solution(mesh):
    rows = P("dom", None)
    one = P("dom")
    whole = P()
    in_specs = (rows, rows, one, one, P("dom", None, None), one) + (whole,) * 10 + (rows, rows)
    split = P(None, "dom", None)
    out_specs = (rows,) * 4 + (split,) * 4
    return jax.shard_map(per_device, mesh=mesh, in_specs=in_specs, out_specs=out_specs, check_vma=False)
```

profile of v0, /device:TPU:1, one launch (start us, length us, event | category | flops | bytes accessed | tf_op | source)
XLA Modules:
  0.0 85.2 jit_solution(13891946724322456599)
XLA Ops:
  1.3 0.8 copy.27
  2.1 0.7 reshape.39.rows_ref
  2.8 14.9 %halo.1.halo_hbm = bf16[128,512]{1,0:T(8,128)(2,1)} custom-call(bf16[512,512]{1,0:T(8,128)(2,1)} %h_hbm.3, s32[1024]{0:T(1024)} %reshape.39.rows_ref), custom_call_target="tpu_custom_call" | custom-call | tf_op jit(solution)/shard_map/halo/pallas_call | solution.py:101
  17.6 28.6 %rows.1 = (bf16[512,512]{1,0:T(8,128)(2,1)}, bf16[2048,512]{1,0:T(8,128)(2,1)}, f32[2048,512]{1,0:T(8,128)}, bf16[2048,512]{1,0:T(8,128)(2,1)}, bf16[2048,512]{1...) custom-call(s32[16,128]{1,0:T(8,128)} %bitcast.11, ...), custom_call_target="tpu_custom_call" | custom-call | tf_op jit(solution)/shard_map/rows/pallas_call | solution.py:276
  46.3 34.6 %sums.1 = (f32[32,512]{1,0:T(8,128)}, bf16[512,512]{1,0:T(8,128)(2,1)}, f32[72,512]{1,0:T(8,128)}) custom-call(s32[16,128]{1,0:T(8,128)} %bitcast.12, s32[16,128]{1,0:T(8,128)} %bitcast.14, bf16[16,96,512]{2,1,0:T(8,128)(2,1)} %get-tuple-element.26.gnode_hbm, bf16[512,512]{1,0:T(8,128)(2,1)} %h_hbm.3, bf16[128,512]{1,0:T(8,128)(2,1)} %halo.1.halo_hbm, ...), custom_call_target="tpu_custom_call" | custom-call | tf_op jit(solution)/shard_map/sums/pallas_call | solution.py:597
  80.9 2.9 %last.1 = (f32[512,512]{1,0:T(8,128)}, f32[1,12,512]{2,1,0:T(8,128)}, f32[1,4,512]{2,1,0:T(4,128)}, f32[1,8,512]{2,1,0:T(8,128)}, f32[1,4,512]{2,1,0:T(4,128)}) custom-call(s32[1024]{0:T(1024)} %reshape.39.rows_ref, f32[32,512]{1,0:T(8,128)} %get-tuple-element.30.sums_ref, bf16[512,512]{1,0:T(8,128)(2,1)} %get-tuple-element.31.part_ref, ...), custom_call_target="tpu_custom_call" | custom-call | tf_op jit(solution)/shard_map/last/pallas_call | solution.py:658
  83.8 1.4 %copy.28 = f32[1,12,512]{2,0,1:T(1,128)} copy(f32[1,12,512]{2,1,0:T(8,128)} %get-tuple-element.52) | data formatting | bytes 49152
where the time goes:
time: 85.5 us; the launch traced here: 85.2 us
  Pallas kernels  81 us (95%)
  local copies, waits for them, and re-layouts  2.86 us (3%)
  between operations  1.31 us (2%)
    pallas_call x1, Pallas kernels, run_sums(): pl.pallas_call(functools.partial(sums_kernel, n_dom), out_shape=[shape((3...  34.6 us
    pallas_call x1, Pallas kernels, run_rows(): pl.pallas_call(functools.partial(rows_kernel, n_dom), out_shape=[shape((N...  28.6 us
    pallas_call x1, Pallas kernels, fetch_halo(): pl.pallas_call(functools.partial(halo_kernel, n_dom), out_shape=jax.Shape...  14.9 us
    pallas_call x1, Pallas kernels, run_last(): pl.pallas_call(functools.partial(last_kernel, n_dom, edge_factor, node_fa...  2.86 us
    unnamed x2, local copies, waits for them, and re-layouts  2.18 us

commit v1 on v0

--- a/solution.py
+++ b/solution.py
@@ -21,9 +21,11 @@
 HALO = SLOTS * HB
 HPAD = 128
 TAB = N + HPAD
-C = 256
+C = 512
 CHUNKS = E // C
 XW = L + TAB + N
+WIDE = L // 2
+LANES = 128
 VMEM_LIMIT = 56 * 1024 * 1024
 
 NT = (((1,), (1,)), ((), ()))
@@ -75,7 +77,7 @@
         pl.semaphore_signal(barrier, inc=1, device_id=(device,), device_id_type=MESH)
     for s in range(SLOTS):
         for k in range(HB):
-            row = rows_ref[targets[s] * HB + k]
+            row = rows_ref[k, targets[s]]
             outgoing[pl.ds(s * HB + k, 1), :] = wide[pl.ds(row, 1), :]
     pl.semaphore_wait(barrier, SLOTS)
     copies = []
@@ -237,8 +239,12 @@
     npart_copy = pltpu.make_async_copy(npart_v, npart_hbm, out_sem.at[1])
     npart_copy.start()
     dy_v[...] = mm_nt(dpre, npin_v[L:, :]).astype(BF)
-    gnode_v[:, 0:64, :] = mm_tn(nx_v[...], dpre).astype(BF).reshape(16, 64, L)
-    gnode_v[:, 64:96, :] = mm_tn(hid, draw).astype(BF).reshape(16, 32, L)
+    grad_in = mm_tn(nx_v[...], dpre).astype(BF)
+    grad_out = mm_tn(hid, draw).astype(BF)
+    for k in range(4):
+        columns = slice(LANES * k, LANES * (k + 1))
+        gnode_v[k, :, 0:64, :] = grad_in[:, columns].reshape(16, 64, LANES)
+        gnode_v[k, :, 64:96, :] = grad_out[:, columns].reshape(16, 32, LANES)
     gnode_copy = pltpu.make_async_copy(gnode_v, gnode_hbm, out_sem.at[2])
     gnode_copy.start()
 
@@ -282,7 +288,7 @@
             shape((E, L), BF),
             shape((E, L), BF),
             shape((E, L), BF),
-            shape((16, 96, L), BF),
+            shape((4, 16, 96, LANES), BF),
             shape((N, L), F32),
         ],
         in_specs=[vmem, vmem, smem, hbm, hbm, hbm, hbm, vmem, hbm, vmem, vmem]
@@ -311,7 +317,7 @@
             pltpu.VMEM((N, L), BF),
             pltpu.VMEM((N, L), BF),
             pltpu.VMEM((N, L), F32),
-            pltpu.VMEM((16, 96, L), BF),
+            pltpu.VMEM((4, 16, 96, LANES), BF),
             dma((7,)),
             dma((CHUNKS,)),
             dma((CHUNKS,)),
@@ -327,18 +333,15 @@
     )(*operands)
 
 
-WIDE = L // 2
-LANES = 128
-
-
 class Wave:
     def __init__(self, coords, refs):
         self.coords = coords
-        (self.own, self.from_core, self.a1, self.b1, self.sa, self.sb, self.a2, self.b2) = refs[:8]
+        (self.own, self.from_core, self.near, self.next, self.sa, self.sb, self.a2, self.b2) = refs[:8]
         self.send, self.recv = refs[8:]
         self.copies = []
 
-    def start(self, src, dst, k, device):
+    def start(self, src, dst, device):
+        k = len(self.copies)
         copy = pltpu.make_async_remote_copy(
             src_ref=src,
             dst_ref=dst,
@@ -350,40 +353,61 @@
         copy.start()
         self.copies.append(copy)
 
-    def to_core(self, src):
+    def pieces(self, k):
         z, x, y, c = self.coords
-        self.start(src, self.from_core, 0, device_at(z, x, y, 1 - c))
+        half = pl.ds(2 * (k % 2), 2)
+        if k // 2 == 0:
+            place, view = z, lambda p: (0, p, half)
+            device = lambda p: device_at(p, x, y, c)
+        else:
+            place, view = x, lambda p: (1, half, p)
+            device = lambda p: device_at(z, p, y, c)
+        low = lax.rem(place, 2)
+        pair = place + 1 - 2 * low
+        cross = lax.rem(place + 3 + 2 * low, 4)
+        near, far = (pair, cross) if k % 2 == 0 else (cross, pair)
+        return view, device, place, near, far
+
+    def to_core(self, src, into=None):
+        z, x, y, c = self.coords
+        self.start(src, self.from_core if into is None else into, device_at(z, x, y, 1 - c))
 
     def first(self):
-        z, x, y, c = self.coords
         self.copies[0].wait_recv()
         own, got = self.own, self.from_core
-        for zz in range(4):
-            own[zz] = (own[zz].astype(F32) + got[zz].astype(F32)).astype(BF)
+        for lanes in range(2):
+            for zz in range(4):
+                own[lanes, zz] = (own[lanes, zz].astype(F32) + got[lanes, zz].astype(F32)).astype(BF)
+        for k in range(4):
+            view, device, place, near, far = self.pieces(k)
+            self.start(own.at[view(near)], self.near.at[k, 0], device(near))
+            self.start(own.at[view(lax.rem(place + 2, 4))], self.near.at[k, 1], device(near))
+
+    def second(self):
+        own = self.own
+        for k in range(4):
+            view, device, place, near, far = self.pieces(k)
+            self.copies[2 + 2 * k].wait_recv()
+            own[view(far)] = (own[view(far)].astype(F32) + self.near[k, 1].astype(F32)).astype(BF)
+            self.start(own.at[view(far)], self.next.at[k], device(far))
+
+    def third(self):
+        z, x, y, c = self.coords
+        for k in range(4):
+            view, device, place, near, far = self.pieces(k)
+            self.copies[1 + 2 * k].wait_recv()
+            self.copies[9 + k].wait_recv()
+            total = self.own[view(place)].astype(F32) + self.near[k, 0].astype(F32) + self.next[k].astype(F32)
+            into = self.sa if k // 2 == 0 else self.sb
+            into[2 * (k % 2) : 2 * (k % 2) + 2] = total.astype(BF)
         for o in range(1, 4):
             zp, xp = lax.rem(z + 4 - o, 4), lax.rem(x + 4 - o, 4)
-            self.start(own.at[zp, :, :, pl.ds(0, LANES)], self.a1.at[o - 1], o, device_at(zp, x, y, c))
-            self.start(own.at[:, xp, :, pl.ds(LANES, LANES)], self.b1.at[o - 1], 3 + o, device_at(z, xp, y, c))
-
-    def second(self):
+            self.start(self.sa.at[xp], self.a2.at[o - 1], device_at(z, xp, y, c))
+            self.start(self.sb.at[zp], self.b2.at[o - 1], device_at(zp, x, y, c))
+
+    def fourth(self, block, at):
         z, x, y, c = self.coords
-        for copy in self.copies[1:7]:
-            copy.wait_recv()
-        a = self.own[z, :, :, 0:LANES].astype(F32)
-        b = self.own[:, x, :, LANES:WIDE].astype(F32)
-        for o in range(3):
-            a = a + self.a1[o].astype(F32)
-            b = b + self.b1[o].astype(F32)
-        self.sa[...] = a.astype(BF)
-        self.sb[...] = b.astype(BF)
-        for o in range(1, 4):
-            zp, xp = lax.rem(z + 4 - o, 4), lax.rem(x + 4 - o, 4)
-            self.start(self.sa.at[xp], self.a2.at[o - 1], 6 + o, device_at(z, xp, y, c))
-            self.start(self.sb.at[zp], self.b2.at[o - 1], 9 + o, device_at(zp, x, y, c))
-
-    def third(self, block, at):
-        z, x, y, c = self.coords
-        for copy in self.copies[7:13]:
+        for copy in self.copies[13:19]:
             copy.wait_recv()
         a, b = self.sa[x].astype(F32), self.sb[z].astype(F32)
         for o in range(3):
@@ -404,16 +428,16 @@
 def wave_scratch(depth):
     dma = pltpu.SemaphoreType.DMA
     return [
-        pltpu.VMEM((4, 4, depth, WIDE), BF),
-        pltpu.VMEM((4, 4, depth, WIDE), BF),
-        pltpu.VMEM((3, 4, depth, LANES), BF),
-        pltpu.VMEM((3, 4, depth, LANES), BF),
+        pltpu.VMEM((2, 4, 4, depth, LANES), BF),
+        pltpu.VMEM((2, 4, 4, depth, LANES), BF),
+        pltpu.VMEM((4, 2, 2, depth, LANES), BF),
+        pltpu.VMEM((4, 2, depth, LANES), BF),
         pltpu.VMEM((4, depth, LANES), BF),
         pltpu.VMEM((4, depth, LANES), BF),
         pltpu.VMEM((3, depth, LANES), BF),
         pltpu.VMEM((3, depth, LANES), BF),
-        dma((13,)),
-        dma((13,)),
+        dma((19,)),
+        dma((19,)),
     ]
 
 
@@ -452,8 +476,9 @@
     load(halo_hbm, tab_v.at[pl.ds(N, HPAD)])
     load(e_hbm, e_v)
     load(dpre_hbm.at[:, mine], dpre_v.at[1])
-    for k in range(4):
-        load(gnode_hbm.at[pl.ds(4 * k, 4), :, mine], node_wave.own.at[k])
+    for lanes in range(2):
+        for k in range(4):
+            load(gnode_hbm.at[2 * c + lanes, pl.ds(4 * k, 4)], node_wave.own.at[lanes, k])
     load(hid_hbm, hid_v)
     load(draw_hbm.at[:, theirs], draw_v.at[0])
     load(draw_hbm.at[:, mine], draw_v.at[1])
@@ -467,12 +492,7 @@
     along += [device_at(z, lax.rem(x + o, 4), y, c) for o in range(1, 4)]
     greet(owners + others + along)
 
-    node_wave.start(
-        gnode_hbm.at[:, :, theirs],
-        node_wave.from_core.reshape(16, 96, WIDE),
-        0,
-        device_at(z, x, y, 1 - c),
-    )
+    node_wave.to_core(gnode_hbm.at[pl.ds(2 * (1 - c), 2)], node_wave.from_core.reshape(2, 16, 96, LANES))
 
     index = table_index(snd_ref[...], me, n_dom)
     high = lax.broadcasted_iota(I32, (TAB, 128), 0)
@@ -485,6 +505,11 @@
 
     for k in range(4):
         loads[k].wait()
+
+    def put_lanes(product, dst, depth):
+        for lanes in range(2):
+            part = product[:, LANES * lanes : LANES * (lanes + 1)]
+            dst[lanes] = part.astype(BF).reshape(4, 4, depth, LANES)
 
     def in_products(half, dst):
         dpre = dpre_v[half]
@@ -495,14 +520,14 @@
         product = jnp.concatenate(
             [mm_tn(e_v[...], dpre), mm_tn(tab_v[...], sent), mm_tn(tab_v[0:N, :], taken)], axis=0
         )
-        dst[...] = product.astype(BF).reshape(4, 4, 96, WIDE)
+        put_lanes(product, dst, 96)
 
     def out_products(half, dst):
-        dst[...] = mm_tn(hid_v[...], draw_v[half]).astype(BF).reshape(4, 4, 32, WIDE)
+        put_lanes(mm_tn(hid_v[...], draw_v[half]), dst, 32)
 
     in_products(0, there_in)
     in_wave.to_core(there_in)
-    for k in range(5, 9):
+    for k in range(5, 13):
         loads[k].wait()
     node_wave.first()
     loads[4].wait()
@@ -510,11 +535,14 @@
     in_wave.first()
     node_wave.second()
 
-    for k in range(9, 16):
+    for k in range(13, 20):
         loads[k].wait()
     out_products(0, there_out)
     out_wave.to_core(there_out)
+    node_wave.third()
+    in_wave.second()
     out_products(1, out_wave.own)
+    out_wave.first()
 
     y_v[...] = mm_nt(as_v[0, N : N + HALO, :], ps_v[0]) + mm_nt(as_v[1, N : N + HALO, :], ps_v[1])
     returns = []
@@ -529,18 +557,18 @@
         )
         copy.start()
         returns.append(copy)
-    out_wave.first()
+    in_wave.third()
+    out_wave.second()
     part_ref[...] = (
         mm_nt(as_v[0, 0:N, :], ps_v[0])
         + mm_nt(as_v[1, 0:N, :], ps_v[1])
         + mm_nt(ar_v[0], pr_v[0])
         + mm_nt(ar_v[1], pr_v[1])
     ).astype(BF)
-    node_wave.third(block, pl.ds(0, 96))
-    in_wave.second()
-    out_wave.second()
-    in_wave.third(block, pl.ds(96, 96))
-    out_wave.third(block, pl.ds(192, 32))
+    out_wave.third()
+    node_wave.fourth(block, pl.ds(0, 96))
+    in_wave.fourth(block, pl.ds(96, 96))
+    out_wave.fourth(block, pl.ds(192, 32))
 
     row = lax.broadcasted_iota(I32, (256, 224), 0)
     col = lax.broadcasted_iota(I32, (256, 224), 1)
@@ -611,13 +639,13 @@
             pltpu.VMEM((N, E), BF),
             pltpu.VMEM((2, TAB, WIDE), BF),
             pltpu.VMEM((2, N, WIDE), BF),
-            pltpu.VMEM((4, 4, 96, WIDE), BF),
-            pltpu.VMEM((4, 4, 32, WIDE), BF),
+            pltpu.VMEM((2, 4, 4, 96, LANES), BF),
+            pltpu.VMEM((2, 4, 4, 32, LANES), BF),
             pltpu.VMEM((HALO, L), F32),
             pltpu.VMEM((224, WIDE), BF),
             pltpu.VMEM((8, 32, WIDE), BF),
             pltpu.VMEM((7, 32, WIDE), BF),
-            dma((16,)),
+            dma((20,)),
             dma((SLOTS,)),
             dma((SLOTS,)),
             dma((7,)),
@@ -643,11 +671,11 @@
     for s in range(SLOTS):
         reader = lax.rem(me - slot_shift(s) + n_dom, n_dom)
         for k in range(HB):
-            at = pl.ds(rows_ref[reader * HB + k], 1)
+            at = pl.ds(rows_ref[k, reader], 1)
             grad_ref[at, :] = grad_ref[at, :] + ret_ref[s * HB + k : s * HB + k + 1, :]
     nin_ref[0] = sums_ref[0:8, :] * node_factor
     nout_ref[0] = sums_ref[8:12, :] * node_factor
-    ein_ref[0] = sums_ref[12:24, :] * edge_factor
+    ein_ref[...] = (sums_ref[12:24, :] * edge_factor).reshape(12, 1, L)
     eout_ref[0] = sums_ref[24:28, :] * edge_factor
 
 
@@ -659,7 +687,7 @@
         functools.partial(last_kernel, n_dom, edge_factor, node_factor),
         out_shape=[
             shape((N, L), F32),
-            shape((1, 12, L), F32),
+            shape((12, 1, L), F32),
             shape((1, 4, L), F32),
             shape((1, 8, L), F32),
             shape((1, 4, L), F32),
@@ -691,7 +719,7 @@
     edge_cot,
 ):
     n_dom = lax.axis_size("dom")
-    slot_rows = send_rows.reshape(-1)
+    slot_rows = send_rows.transpose(0, 2, 1).reshape(HB, n_dom)
     snd = sender_index.reshape(E // 128, 128)
     rcv = receiver_index.reshape(E // 128, 128)
     pin, pout = edge_proj_in.reshape(3 * L, L), edge_proj_out.reshape(L, L)
@@ -709,6 +737,7 @@
     node_grad, edge_in, edge_out_grad, node_in, node_out_grad = run_last(
         n_dom, edge_factor, node_factor, slot_rows, sums, part, returned, npart
     )
+    edge_in = edge_in.transpose(1, 0, 2)
     return node_out, edge_out, node_grad, edge_grad, edge_in, edge_out_grad, node_in, node_out_grad
 
 

time: 85.5 us -> 81.9 us (0.958)
  local copies, waits for them, and re-layouts: 2.86 us -> 0 us
  Pallas kernels: 81 us -> 79.9 us
    pallas_call x1, Pallas kernels: 28.6 us -> 24.5 us  [run_rows(): pl.pallas_call(functools.partial(rows_kernel, n_dom), out_shape=[shape((N...]
    pallas_call x1, Pallas kernels: 34.6 us -> 37.6 us  [run_sums(): pl.pallas_call(functools.partial(sums_kernel, n_dom), out_shape=[shape((3...]
    unnamed x2 -> x0, local copies, waits for them, and re-layouts: 2.18 us -> none
where the time goes in v1:
time: 81.9 us; the launch traced here: 81.2 us
  Pallas kernels  79.9 us (98%)
  between operations  1.3 us (2%)
    pallas_call x1, Pallas kernels, run_sums(): pl.pallas_call(functools.partial(sums_kernel, n_dom), out_shape=[shape((3...  37.6 us
    pallas_call x1, Pallas kernels, run_rows(): pl.pallas_call(functools.partial(rows_kernel, n_dom), out_shape=[shape((N...  24.5 us
    pallas_call x1, Pallas kernels, fetch_halo(): pl.pallas_call(functools.partial(halo_kernel, n_dom), out_shape=jax.Shape...  14.9 us
    pallas_call x1, Pallas kernels, run_last(): pl.pallas_call(functools.partial(last_kernel, n_dom, edge_factor, node_fa...  2.85 us

profile of v1, /device:TPU:1, one launch (start us, length us, event | category | flops | bytes accessed | tf_op | source)
XLA Modules:
  0.0 81.2 jit_solution(1924911322199933765)
XLA Ops:
  1.3 14.9 %halo.1.halo_hbm = bf16[128,512]{1,0:T(8,128)(2,1)} custom-call(bf16[512,512]{1,0:T(8,128)(2,1)} %h_hbm.3, s32[8,128]{1,0:T(8,128)} %bitcast.19), custom_call_target="tpu_custom_call" | custom-call | tf_op jit(solution)/shard_map/halo/pallas_call | solution.py:103
  16.2 24.5 %rows.1 = (bf16[512,512]{1,0:T(8,128)(2,1)}, bf16[2048,512]{1,0:T(8,128)(2,1)}, f32[2048,512]{1,0:T(8,128)}, bf16[2048,512]{1,0:T(8,128)(2,1)}, bf16[2048,512]{1...) custom-call(s32[16,128]{1,0:T(8,128)} %bitcast.15, ...), custom_call_target="tpu_custom_call" | custom-call | tf_op jit(solution)/shard_map/rows/pallas_call | solution.py:282
  40.8 37.6 %sums.1 = (f32[32,512]{1,0:T(8,128)}, bf16[512,512]{1,0:T(8,128)(2,1)}, f32[72,512]{1,0:T(8,128)}) custom-call(s32[16,128]{1,0:T(8,128)} %bitcast.16, s32[16,128]{1,0:T(8,128)} %bitcast.18, bf16[4,16,96,128]{3,2,1,0:T(8,128)(2,1)} %get-tuple-element.26.gnode_hbm, bf16[512,512]{1,0:T(8,128)(2,1)} %h_hbm.3, bf16[128,512]{1,0:T(8,128)(2,1)} %halo.1.halo_hbm, ...), custom_call_target="tpu_custom_call" | custom-call | tf_op jit(solution)/shard_map/sums/pallas_call | solution.py:625
  78.3 2.8 %last.1 = (f32[512,512]{1,0:T(8,128)}, f32[12,1,512]{2,1,0:T(1,128)}, f32[1,4,512]{2,1,0:T(4,128)}, f32[1,8,512]{2,1,0:T(8,128)}, f32[1,4,512]{2,1,0:T(4,128)}) custom-call(s32[8,128]{1,0:T(8,128)} %bitcast.20, f32[32,512]{1,0:T(8,128)} %get-tuple-element.30.sums_ref, bf16[512,512]{1,0:T(8,128)(2,1)} %get-tuple-element.31.part_ref, ...), custom_call_target="tpu_custom_call" | custom-call | tf_op jit(solution)/shard_map/last/pallas_call | solution.py:686

commit v2 on v1

--- a/solution.py
+++ b/solution.py
@@ -23,7 +23,6 @@
 TAB = N + HPAD
 C = 512
 CHUNKS = E // C
-XW = L + TAB + N
 WIDE = L // 2
 LANES = 128
 VMEM_LIMIT = 56 * 1024 * 1024
@@ -68,13 +67,43 @@
     pl.semaphore_wait(barrier, len(devices))
 
 
-def halo_kernel(n_dom, h_ref, rows_ref, out_ref, wide, outgoing, incoming, send_sem, recv_sem):
+def one_hot_columns(index, lane, blocks):
+    column = jnp.broadcast_to(index, (128, 128)).T
+    return jnp.concatenate(
+        [(column == lane + 128 * m).astype(F32).astype(BF) for m in range(blocks)], axis=1
+    )
+
+
+def halo_kernel(
+    n_dom,
+    snd_ref, rcv_ref, rows_ref, h_hbm, e_hbm, pin_hbm, b_in,
+    halo_ref, thalo_ref, pre_hbm,
+    h_v, x_v, pin_v, t_v, pre_v, wide, outgoing, incoming,
+    in_sem, e_sem, pre_sem, send_sem, recv_sem,
+):
     me = lax.axis_index("dom")
     targets = [lax.rem(me - slot_shift(s) + n_dom, n_dom) for s in range(SLOTS)]
-    wide[...] = h_ref[...].astype(F32)
+
+    def rows(i):
+        return pl.ds(pl.multiple_of(i * C, C), C)
+
+    def e_load(i):
+        return pltpu.make_async_copy(e_hbm.at[rows(i)], x_v.at[rows(i), pl.ds(0, L)], e_sem.at[i])
+
+    def pre_put(i):
+        return pltpu.make_async_copy(pre_v.at[rows(i)], pre_hbm.at[rows(i)], pre_sem.at[i])
+
     barrier = pltpu.get_barrier_semaphore()
     for device in targets:
         pl.semaphore_signal(barrier, inc=1, device_id=(device,), device_id_type=MESH)
+    h_load = pltpu.make_async_copy(h_hbm, h_v, in_sem.at[0])
+    h_load.start()
+    pin_load = pltpu.make_async_copy(pin_hbm, pin_v, in_sem.at[1])
+    pin_load.start()
+    for i in range(CHUNKS):
+        e_load(i).start()
+    h_load.wait()
+    wide[...] = h_v[...].astype(F32)
     for s in range(SLOTS):
         for k in range(HB):
             row = rows_ref[k, targets[s]]
@@ -92,32 +121,65 @@
         )
         copy.start()
         copies.append(copy)
+
+    pin_load.wait()
+    t_v[0:L, :] = pin_v[0:L, :]
+    t_v[L : 2 * L, :] = mm(h_v[...], pin_v[L : 2 * L, :]).astype(BF)
+    t_v[2 * L :, :] = (mm(h_v[...], pin_v[2 * L :, :]) + b_in[...]).astype(BF)
+    lane = lax.broadcasted_iota(I32, (128, 128), 1)
+
+    def local(i, carry):
+        for b in range(C // 128):
+            block = i * (C // 128) + b
+            at = pl.ds(pl.multiple_of(block * 128, 128), 128)
+            x_v[at, L : 2 * L] = one_hot_columns(snd_ref[pl.ds(block, 1), :], lane, N // 128)
+            x_v[at, 2 * L :] = one_hot_columns(rcv_ref[pl.ds(block, 1), :], lane, N // 128)
+        e_load(i).wait()
+        pre_v[rows(i), :] = mm(x_v[rows(i), :], t_v[...]).astype(BF)
+        pre_put(i).start()
+        return carry
+
+    lax.fori_loop(0, CHUNKS, local, 0)
     for copy in copies:
         copy.wait()
-    out_ref[...] = jnp.concatenate(
-        [incoming[...].astype(BF), jnp.zeros((HPAD - HALO, L), BF)], axis=0
-    )
-
-
-def fetch_halo(node_rows, slot_rows, n_dom):
+    halo = jnp.concatenate([incoming[...].astype(BF), jnp.zeros((HPAD - HALO, L), BF)], axis=0)
+    halo_ref[...] = halo
+    thalo_ref[...] = mm(halo, pin_v[L : 2 * L, :]).astype(BF)
+    for i in range(CHUNKS):
+        pre_put(i).wait()
+
+
+def run_halo(n_dom, *operands):
+    hbm = pl.BlockSpec(memory_space=pl.ANY)
+    vmem = pl.BlockSpec(memory_space=pltpu.VMEM)
+    smem = pl.BlockSpec(memory_space=pltpu.SMEM)
+    shape = jax.ShapeDtypeStruct
+    dma = pltpu.SemaphoreType.DMA
     return pl.pallas_call(
         functools.partial(halo_kernel, n_dom),
-        out_shape=jax.ShapeDtypeStruct((HPAD, L), BF),
-        in_specs=[
-            pl.BlockSpec(memory_space=pltpu.VMEM),
-            pl.BlockSpec(memory_space=pltpu.SMEM),
-        ],
-        out_specs=pl.BlockSpec(memory_space=pltpu.VMEM),
+        out_shape=[shape((HPAD, L), BF), shape((HPAD, L), BF), shape((E, L), BF)],
+        in_specs=[vmem, vmem, smem, hbm, hbm, hbm, vmem],
+        out_specs=[vmem, vmem, hbm],
         scratch_shapes=[
+            pltpu.VMEM((N, L), BF),
+            pltpu.VMEM((E, 3 * L), BF),
+            pltpu.VMEM((3 * L, L), BF),
+            pltpu.VMEM((3 * L, L), BF),
+            pltpu.VMEM((E, L), BF),
             pltpu.VMEM((N, L), F32),
             pltpu.VMEM((HALO, L), F32),
             pltpu.VMEM((HALO, L), F32),
-            pltpu.SemaphoreType.DMA((SLOTS,)),
-            pltpu.SemaphoreType.DMA((SLOTS,)),
+            dma((2,)),
+            dma((CHUNKS,)),
+            dma((CHUNKS,)),
+            dma((SLOTS,)),
+            dma((SLOTS,)),
         ],
-        compiler_params=pltpu.CompilerParams(collective_id=0, has_side_effects=True),
+        compiler_params=pltpu.CompilerParams(
+            collective_id=0, has_side_effects=True, vmem_limit_bytes=VMEM_LIMIT
+        ),
         name="halo",
-    )(node_rows, slot_rows)
+    )(*operands)
 
 
 def norm_forward(raw):
@@ -139,12 +201,12 @@
 
 def rows_kernel(
     n_dom,
-    snd_ref, rcv_ref, cnt_ref, h_hbm, halo_hbm, e_hbm, pin_hbm, b_in, pout_hbm, b_out, gain,
+    snd_ref, rcv_ref, cnt_ref, thalo_ref, h_hbm, part_hbm, e_hbm, pin_hbm, pout_hbm, b_out, gain,
     npin_hbm, nb_in, npout_hbm, nb_out, ngain, ncot_hbm, ecot_hbm,
     nout_hbm, eout_hbm, egrad_hbm, dpre_hbm, draw_hbm, hid_hbm, gnode_hbm, npart_hbm,
-    idx_v, x_v, rt_v, w_v, tab_v, pin_v, pout_v, npin_v, npout_v, ncot_v, cot_v,
+    idx_v, x_v, rt_v, e_v, part_v, h_v, pe_v, pout_v, npin_v, npout_v, ncot_v, cot_v,
     pre_v, hid_v, n_v, inv_v, enew_v, draw_v, dpre_v, nx_v, dy_v, nout_v, npart_v, gnode_v,
-    in_sem, e_sem, cot_sem, eout_sem, hid_sem, draw_sem, dpre_sem, egrad_sem, out_sem,
+    in_sem, e_sem, part_sem, cot_sem, eout_sem, hid_sem, draw_sem, dpre_sem, egrad_sem, out_sem,
 ):
     me = lax.axis_index("dom")
 
@@ -155,7 +217,10 @@
         return pl.ds(pl.multiple_of(i * C, C), C)
 
     def e_load(i):
-        return pltpu.make_async_copy(e_hbm.at[rows(i)], x_v.at[rows(i), pl.ds(0, L)], e_sem.at[i])
+        return pltpu.make_async_copy(e_hbm.at[rows(i)], e_v.at[rows(i)], e_sem.at[i])
+
+    def part_load(i):
+        return pltpu.make_async_copy(part_hbm.at[rows(i)], part_v.at[rows(i)], part_sem.at[i])
 
     def cot_load(i):
         return pltpu.make_async_copy(ecot_hbm.at[rows(i)], cot_v.at[rows(i)], cot_sem.at[i])
@@ -164,19 +229,20 @@
         return pltpu.make_async_copy(src.at[rows(i)], dst.at[rows(i)], sem.at[i])
 
     loads = [
-        load(0, h_hbm, tab_v.at[pl.ds(0, N)]),
-        load(1, halo_hbm, tab_v.at[pl.ds(N, HPAD)]),
-        load(2, pin_hbm, pin_v),
-        load(3, pout_hbm, pout_v),
-        load(4, npin_hbm, npin_v),
-        load(5, npout_hbm, npout_v),
-        load(6, ncot_hbm, ncot_v),
+        load(0, pout_hbm, pout_v),
+        load(1, h_hbm, h_v),
+        load(2, npin_hbm, npin_v),
+        load(3, npout_hbm, npout_v),
+        load(4, ncot_hbm, ncot_v),
+        load(5, pin_hbm.at[pl.ds(0, L)], pe_v),
     ]
-    for k in range(3):
-        loads[k].start()
+    part_load(0).start()
+    loads[0].start()
     for i in range(CHUNKS):
         e_load(i).start()
-    for k in range(3, 7):
+        if i + 1 < CHUNKS:
+            part_load(i + 1).start()
+    for k in range(1, 6):
         loads[k].start()
     for i in range(CHUNKS):
         cot_load(i).start()
@@ -184,30 +250,18 @@
     idx_v[...] = table_index(snd_ref[...], me, n_dom)
     lane = lax.broadcasted_iota(I32, (128, 128), 1)
     high = lax.broadcasted_iota(I32, (N, 128), 0)
-
-    for k in range(3):
-        loads[k].wait()
-    w_v[0:L, :] = pin_v[0:L, :]
-    w_v[L : L + TAB, :] = mm(tab_v[...], pin_v[L : 2 * L, :]).astype(BF)
-    w_v[L + TAB :, :] = (mm(tab_v[0:N, :], pin_v[2 * L :, :]) + b_in[...]).astype(BF)
-    loads[3].wait()
+    loads[0].wait()
 
     def forward(i, carry):
-        e_load(i).wait()
         for b in range(C // 128):
             block = i * (C // 128) + b
             at = pl.ds(pl.multiple_of(block * 128, 128), 128)
-            s_col = jnp.broadcast_to(idx_v[pl.ds(block, 1), :], (128, 128)).T
             r_row = rcv_ref[pl.ds(block, 1), :]
-            r_col = jnp.broadcast_to(r_row, (128, 128)).T
-            for m in range(TAB // 128):
-                x_v[at, L + 128 * m : L + 128 * (m + 1)] = (s_col == lane + 128 * m).astype(F32).astype(BF)
-            for m in range(N // 128):
-                x_v[at, L + TAB + 128 * m : L + TAB + 128 * (m + 1)] = (
-                    (r_col == lane + 128 * m).astype(F32).astype(BF)
-                )
+            x_v[at, 0:HPAD] = one_hot_columns(idx_v[pl.ds(block, 1), :] - N, lane, 1)
+            x_v[at, HPAD:] = one_hot_columns(r_row, lane, N // 128)
             rt_v[:, at] = (jnp.broadcast_to(r_row, (N, 128)) == high).astype(F32).astype(BF)
-        pre = mm(x_v[rows(i), :], w_v[...])
+        part_load(i).wait()
+        pre = part_v[rows(i), :].astype(F32) + mm(x_v[rows(i), 0:HPAD], thalo_ref[...])
         pre_v[rows(i), :] = pre
         hid = (pre * sigmoid(pre)).astype(BF)
         hid_v[rows(i), :] = hid
@@ -215,7 +269,8 @@
         normed, inv = norm_forward(raw)
         n_v[rows(i), :] = normed
         inv_v[rows(i), :] = inv
-        enew_v[rows(i), :] = (x_v[rows(i), 0:L].astype(F32) + normed * gain[...]).astype(BF)
+        e_load(i).wait()
+        enew_v[rows(i), :] = (e_v[rows(i), :].astype(F32) + normed * gain[...]).astype(BF)
         put(i, enew_v, eout_hbm, eout_sem).start()
         put(i, hid_v, hid_hbm, hid_sem).start()
         return carry
@@ -223,14 +278,14 @@
     lax.fori_loop(0, CHUNKS, forward, 0)
 
     valid = (lax.broadcasted_iota(I32, (N, 1), 0) < cnt_ref[0]).astype(F32)
-    nx_v[:, 0:L] = tab_v[0:N, :]
     nx_v[:, L:] = (mm(rt_v[...], enew_v[...]) * valid).astype(BF)
-    for k in range(4, 7):
+    for k in range(1, 6):
         loads[k].wait()
+    nx_v[:, 0:L] = h_v[...]
     pre = mm(nx_v[...], npin_v[...]) + nb_in[...]
     hid = (pre * sigmoid(pre)).astype(BF)
     normed, inv = norm_forward(mm(hid, npout_v[...]) + nb_out[...])
-    nout_v[...] = (tab_v[0:N, :].astype(F32) + valid * (normed * ngain[...])).astype(BF)
+    nout_v[...] = (h_v[...].astype(F32) + valid * (normed * ngain[...])).astype(BF)
     nout_copy = pltpu.make_async_copy(nout_v, nout_hbm, out_sem.at[0])
     nout_copy.start()
     draw = norm_backward(valid * ncot_v[...] * ngain[...], normed, inv).astype(BF)
@@ -250,14 +305,14 @@
 
     def backward(i, carry):
         cot_load(i).wait()
-        total = cot_v[rows(i), :] + mm(x_v[rows(i), L + TAB :], dy_v[...])
+        total = cot_v[rows(i), :] + mm(x_v[rows(i), HPAD:], dy_v[...])
         draw = norm_backward(total * gain[...], n_v[rows(i), :], inv_v[rows(i), :]).astype(BF)
         draw_v[rows(i), :] = draw
         put(i, draw_v, draw_hbm, draw_sem).start()
         dpre = (mm_nt(draw, pout_v[...]) * act_slope(pre_v[rows(i), :])).astype(BF)
         dpre_v[rows(i), :] = dpre
         put(i, dpre_v, dpre_hbm, dpre_sem).start()
-        cot_v[rows(i), :] = total + mm_nt(dpre, pin_v[0:L, :])
+        cot_v[rows(i), :] = total + mm_nt(dpre, pe_v[...])
         put(i, cot_v, egrad_hbm, egrad_sem).start()
         return carry
 
@@ -291,16 +346,17 @@
             shape((4, 16, 96, LANES), BF),
             shape((N, L), F32),
         ],
-        in_specs=[vmem, vmem, smem, hbm, hbm, hbm, hbm, vmem, hbm, vmem, vmem]
+        in_specs=[vmem, vmem, smem, vmem, hbm, hbm, hbm, hbm, hbm, vmem, vmem]
         + [hbm, vmem, hbm, vmem, vmem, hbm, hbm],
         out_specs=[hbm] * 8,
         scratch_shapes=[
             pltpu.VMEM((16, 128), I32),
-            pltpu.VMEM((E, XW), BF),
+            pltpu.VMEM((E, HPAD + N), BF),
             pltpu.VMEM((N, E), BF),
-            pltpu.VMEM((XW, L), BF),
-            pltpu.VMEM((TAB, L), BF),
-            pltpu.VMEM((3 * L, L), BF),
+            pltpu.VMEM((E, L), BF),
+            pltpu.VMEM((E, L), BF),
+            pltpu.VMEM((N, L), BF),
+            pltpu.VMEM((L, L), BF),
             pltpu.VMEM((L, L), BF),
             pltpu.VMEM((2 * L, L), BF),
             pltpu.VMEM((L, L), BF),
@@ -318,7 +374,8 @@
             pltpu.VMEM((N, L), BF),
             pltpu.VMEM((N, L), F32),
             pltpu.VMEM((4, 16, 96, LANES), BF),
-            dma((7,)),
+            dma((6,)),
+            dma((CHUNKS,)),
             dma((CHUNKS,)),
             dma((CHUNKS,)),
             dma((CHUNKS,)),
@@ -336,7 +393,7 @@
 class Wave:
     def __init__(self, coords, refs):
         self.coords = coords
-        (self.own, self.from_core, self.near, self.next, self.sa, self.sb, self.a2, self.b2) = refs[:8]
+        (self.own, self.from_core, self.a1, self.b1, self.sa, self.sb, self.a2, self.b2) = refs[:8]
         self.send, self.recv = refs[8:]
         self.copies = []
 
@@ -353,61 +410,49 @@
         copy.start()
         self.copies.append(copy)
 
-    def pieces(self, k):
-        z, x, y, c = self.coords
-        half = pl.ds(2 * (k % 2), 2)
-        if k // 2 == 0:
-            place, view = z, lambda p: (0, p, half)
-            device = lambda p: device_at(p, x, y, c)
-        else:
-            place, view = x, lambda p: (1, half, p)
-            device = lambda p: device_at(z, p, y, c)
-        low = lax.rem(place, 2)
-        pair = place + 1 - 2 * low
-        cross = lax.rem(place + 3 + 2 * low, 4)
-        near, far = (pair, cross) if k % 2 == 0 else (cross, pair)
-        return view, device, place, near, far
-
     def to_core(self, src, into=None):
         z, x, y, c = self.coords
         self.start(src, self.from_core if into is None else into, device_at(z, x, y, 1 - c))
 
     def first(self):
+        z, x, y, c = self.coords
         self.copies[0].wait_recv()
         own, got = self.own, self.from_core
-        for lanes in range(2):
-            for zz in range(4):
-                own[lanes, zz] = (own[lanes, zz].astype(F32) + got[lanes, zz].astype(F32)).astype(BF)
-        for k in range(4):
-            view, device, place, near, far = self.pieces(k)
-            self.start(own.at[view(near)], self.near.at[k, 0], device(near))
-            self.start(own.at[view(lax.rem(place + 2, 4))], self.near.at[k, 1], device(near))
+        for zz in range(4):
+            own[0, zz] = (own[0, zz].astype(F32) + got[0, zz].astype(F32)).astype(BF)
+        for o in (2, 1, 3):
+            zp = lax.rem(z + 4 - o, 4)
+            self.start(own.at[0, zp], self.a1.at[o - 1], device_at(zp, x, y, c))
+        for zz in range(4):
+            own[1, zz] = (own[1, zz].astype(F32) + got[1, zz].astype(F32)).astype(BF)
+        for o in (2, 1, 3):
+            xp = lax.rem(x + 4 - o, 4)
+            self.start(own.at[1, :, xp], self.b1.at[o - 1], device_at(z, xp, y, c))
 
     def second(self):
-        own = self.own
-        for k in range(4):
-            view, device, place, near, far = self.pieces(k)
-            self.copies[2 + 2 * k].wait_recv()
-            own[view(far)] = (own[view(far)].astype(F32) + self.near[k, 1].astype(F32)).astype(BF)
-            self.start(own.at[view(far)], self.next.at[k], device(far))
-
-    def third(self):
         z, x, y, c = self.coords
-        for k in range(4):
-            view, device, place, near, far = self.pieces(k)
-            self.copies[1 + 2 * k].wait_recv()
-            self.copies[9 + k].wait_recv()
-            total = self.own[view(place)].astype(F32) + self.near[k, 0].astype(F32) + self.next[k].astype(F32)
-            into = self.sa if k // 2 == 0 else self.sb
-            into[2 * (k % 2) : 2 * (k % 2) + 2] = total.astype(BF)
-        for o in range(1, 4):
-            zp, xp = lax.rem(z + 4 - o, 4), lax.rem(x + 4 - o, 4)
+        for copy in self.copies[1:4]:
+            copy.wait_recv()
+        a = self.own[0, z].astype(F32)
+        for o in range(3):
+            a = a + self.a1[o].astype(F32)
+        self.sa[...] = a.astype(BF)
+        for o in (2, 1, 3):
+            xp = lax.rem(x + 4 - o, 4)
             self.start(self.sa.at[xp], self.a2.at[o - 1], device_at(z, xp, y, c))
+        for copy in self.copies[4:7]:
+            copy.wait_recv()
+        b = self.own[1, :, x].astype(F32)
+        for o in range(3):
+            b = b + self.b1[o].astype(F32)
+        self.sb[...] = b.astype(BF)
+        for o in (2, 1, 3):
+            zp = lax.rem(z + 4 - o, 4)
             self.start(self.sb.at[zp], self.b2.at[o - 1], device_at(zp, x, y, c))
 
-    def fourth(self, block, at):
+    def third(self, block, at):
         z, x, y, c = self.coords
-        for copy in self.copies[13:19]:
+        for copy in self.copies[7:13]:
             copy.wait_recv()
         a, b = self.sa[x].astype(F32), self.sb[z].astype(F32)
         for o in range(3):
@@ -430,14 +475,14 @@
     return [
         pltpu.VMEM((2, 4, 4, depth, LANES), BF),
         pltpu.VMEM((2, 4, 4, depth, LANES), BF),
-        pltpu.VMEM((4, 2, 2, depth, LANES), BF),
-        pltpu.VMEM((4, 2, depth, LANES), BF),
+        pltpu.VMEM((3, 4, depth, LANES), BF),
+        pltpu.VMEM((3, 4, depth, LANES), BF),
         pltpu.VMEM((4, depth, LANES), BF),
         pltpu.VMEM((4, depth, LANES), BF),
         pltpu.VMEM((3, depth, LANES), BF),
         pltpu.VMEM((3, depth, LANES), BF),
-        dma((19,)),
-        dma((19,)),
+        dma((13,)),
+        dma((13,)),
     ]
 
 
@@ -475,10 +520,10 @@
     load(h_hbm, tab_v.at[pl.ds(0, N)])
     load(halo_hbm, tab_v.at[pl.ds(N, HPAD)])
     load(e_hbm, e_v)
-    load(dpre_hbm.at[:, mine], dpre_v.at[1])
     for lanes in range(2):
         for k in range(4):
             load(gnode_hbm.at[2 * c + lanes, pl.ds(4 * k, 4)], node_wave.own.at[lanes, k])
+    load(dpre_hbm.at[:, mine], dpre_v.at[1])
     load(hid_hbm, hid_v)
     load(draw_hbm.at[:, theirs], draw_v.at[0])
     load(draw_hbm.at[:, mine], draw_v.at[1])
@@ -502,9 +547,6 @@
         rt_v[:, at] = (
             (jnp.broadcast_to(rcv_ref[k : k + 1, :], (N, 128)) == high[0:N, :]).astype(F32).astype(BF)
         )
-
-    for k in range(4):
-        loads[k].wait()
 
     def put_lanes(product, dst, depth):
         for lanes in range(2):
@@ -525,22 +567,21 @@
     def out_products(half, dst):
         put_lanes(mm_tn(hid_v[...], draw_v[half]), dst, 32)
 
+    for k in range(4):
+        loads[k].wait()
     in_products(0, there_in)
     in_wave.to_core(there_in)
-    for k in range(5, 13):
+    for k in range(4, 12):
         loads[k].wait()
     node_wave.first()
-    loads[4].wait()
+    loads[12].wait()
     in_products(1, in_wave.own)
     in_wave.first()
-    node_wave.second()
-
     for k in range(13, 20):
         loads[k].wait()
     out_products(0, there_out)
     out_wave.to_core(there_out)
-    node_wave.third()
-    in_wave.second()
+    node_wave.second()
     out_products(1, out_wave.own)
     out_wave.first()
 
@@ -557,18 +598,17 @@
         )
         copy.start()
         returns.append(copy)
-    in_wave.third()
-    out_wave.second()
+    in_wave.second()
     part_ref[...] = (
         mm_nt(as_v[0, 0:N, :], ps_v[0])
         + mm_nt(as_v[1, 0:N, :], ps_v[1])
         + mm_nt(ar_v[0], pr_v[0])
         + mm_nt(ar_v[1], pr_v[1])
     ).astype(BF)
-    out_wave.third()
-    node_wave.fourth(block, pl.ds(0, 96))
-    in_wave.fourth(block, pl.ds(96, 96))
-    out_wave.fourth(block, pl.ds(192, 32))
+    node_wave.third(block, pl.ds(0, 96))
+    out_wave.second()
+    in_wave.third(block, pl.ds(96, 96))
+    out_wave.third(block, pl.ds(192, 32))
 
     row = lax.broadcasted_iota(I32, (256, 224), 0)
     col = lax.broadcasted_iota(I32, (256, 224), 1)
@@ -723,9 +763,11 @@
     snd = sender_index.reshape(E // 128, 128)
     rcv = receiver_index.reshape(E // 128, 128)
     pin, pout = edge_proj_in.reshape(3 * L, L), edge_proj_out.reshape(L, L)
-    halo = fetch_halo(node_latent, slot_rows, n_dom)
+    halo, thalo, pre_part = run_halo(
+        n_dom, snd, rcv, slot_rows, node_latent, edge_latent, pin, edge_bias_in
+    )
     node_out, edge_out, edge_grad, dpre, draw, hid, gnode, npart = run_rows(
-        n_dom, snd, rcv, node_count, node_latent, halo, edge_latent, pin, edge_bias_in, pout,
+        n_dom, snd, rcv, node_count, thalo, node_latent, pre_part, edge_latent, pin, pout,
         edge_bias_out, edge_gain, node_proj_in.reshape(2 * L, L), node_bias_in,
         node_proj_out.reshape(L, L), node_bias_out, node_gain, node_cot, edge_cot,
     )

time: 81.9 us -> 74.1 us (0.905)
  Pallas kernels: 79.9 us -> 72.5 us
    pallas_call x1, Pallas kernels: 37.6 us -> 31 us  [run_sums(): pl.pallas_call(functools.partial(sums_kernel, n_dom), out_shape=[shape((3...]
    pallas_call x1, Pallas kernels: 24.5 us -> 20.5 us  [run_rows(): pl.pallas_call(functools.partial(rows_kernel, n_dom), out_shape=[shape((N...]
    pallas_call x1, Pallas kernels: 14.9 us -> 18.2 us  [run_halo(): pl.pallas_call(functools.partial(halo_kernel, n_dom), out_shape=[shape((H...]
where the time goes in v2:
time: 74.1 us; the launch traced here: 73.8 us
  Pallas kernels  72.5 us (98%)
  between operations  1.3 us (2%)
    pallas_call x1, Pallas kernels, run_sums(): pl.pallas_call(functools.partial(sums_kernel, n_dom), out_shape=[shape((3...  31 us
    pallas_call x1, Pallas kernels, run_rows(): pl.pallas_call(functools.partial(rows_kernel, n_dom), out_shape=[shape((N...  20.5 us
    pallas_call x1, Pallas kernels, run_halo(): pl.pallas_call(functools.partial(halo_kernel, n_dom), out_shape=[shape((H...  18.2 us
    pallas_call x1, Pallas kernels, run_last(): pl.pallas_call(functools.partial(last_kernel, n_dom, edge_factor, node_fa...  2.85 us

profile of v2, /device:TPU:1, one launch (start us, length us, event | category | flops | bytes accessed | tf_op | source)
XLA Modules:
  0.0 73.8 jit_solution(4326576049880475577)
XLA Ops:
  1.3 18.2 %halo.1 = (bf16[128,512]{1,0:T(8,128)(2,1)}, bf16[128,512]{1,0:T(8,128)(2,1)}, bf16[2048,512]{1,0:T(8,128)(2,1)}) custom-call(s32[16,128]{1,0:T(8,128)} %bitcast.16, s32[16,128]{1,0:T(8,128)} %bitcast.19, s32[8,128]{1,0:T(8,128)} %bitcast.22, bf16[512,512]{1,0:T(8,128)(2,1)} %h_hbm.5, bf16[2048,512]{1,0:T(8,128)(2,1)} %e_hbm.5, bf16[1536,512]{1,0:T(8,128)(2,1)} %bitcast.10, ...), custom_call_target="tpu_custom_call" | custom-call | tf_op jit(solution)/shard_map/halo/pallas_call | solution.py:158
  19.5 20.5 %rows.1 = (bf16[512,512]{1,0:T(8,128)(2,1)}, bf16[2048,512]{1,0:T(8,128)(2,1)}, f32[2048,512]{1,0:T(8,128)}, bf16[2048,512]{1,0:T(8,128)(2,1)}, bf16[2048,512]{1...) custom-call(s32[16,128]{1,0:T(8,128)} %bitcast.17, ...), custom_call_target="tpu_custom_call" | custom-call | tf_op jit(solution)/shard_map/rows/pallas_call | solution.py:337
  40.0 31.0 %sums.1 = (f32[32,512]{1,0:T(8,128)}, bf16[512,512]{1,0:T(8,128)(2,1)}, f32[72,512]{1,0:T(8,128)}) custom-call(s32[16,128]{1,0:T(8,128)} %bitcast.18, s32[16,128]{1,0:T(8,128)} %bitcast.21, bf16[4,16,96,128]{3,2,1,0:T(8,128)(2,1)} %get-tuple-element.31.gnode_hbm, bf16[512,512]{1,0:T(8,128)(2,1)} %h_hbm.5, bf16[128,512]{1,0:T(8,128)(2,1)} %get-tuple-element.32.halo_hbm, ...), custom_call_target="tpu_custom_call" | custom-call | tf_op jit(solution)/shard_map/sums/pallas_call | solution.py:665
  71.0 2.8 %last.1 = (f32[512,512]{1,0:T(8,128)}, f32[12,1,512]{2,1,0:T(1,128)}, f32[1,4,512]{2,1,0:T(4,128)}, f32[1,8,512]{2,1,0:T(8,128)}, f32[1,4,512]{2,1,0:T(4,128)}) custom-call(s32[8,128]{1,0:T(8,128)} %bitcast.23, f32[32,512]{1,0:T(8,128)} %get-tuple-element.36.sums_ref, bf16[512,512]{1,0:T(8,128)(2,1)} %get-tuple-element.37.part_ref, ...), custom_call_target="tpu_custom_call" | custom-call | tf_op jit(solution)/shard_map/last/pallas_call | solution.py:726

commit v3 on v2

--- a/solution.py
+++ b/solution.py
@@ -23,6 +23,7 @@
 TAB = N + HPAD
 C = 512
 CHUNKS = E // C
+S = 256
 WIDE = L // 2
 LANES = 128
 VMEM_LIMIT = 56 * 1024 * 1024
@@ -45,6 +46,17 @@
 
 def mm_tn(a, b):
     return lax.dot_general(a, b, TN, preferred_element_type=F32)
+
+
+def staggered(*streams):
+    live = list(streams)
+    turn = 0
+    while live:
+        for stream in live[: turn + 1]:
+            if next(stream, StopIteration) is StopIteration:
+                live.remove(stream)
+                turn -= 1
+        turn += 1
 
 
 def sigmoid(x):
@@ -60,6 +72,17 @@
     return jnp.where(sender < N, sender, N + slot * HB + row)
 
 
+def boundary_rows(rows_ref, readers):
+    lane = lax.broadcasted_iota(I32, (HB, 128), 1)
+    node = lax.broadcasted_iota(I32, (HB, N), 1)
+    listed = rows_ref[...]
+    picked = []
+    for reader in readers:
+        column = jnp.sum(jnp.where(lane == reader, listed, 0), axis=1, keepdims=True)
+        picked.append((jnp.broadcast_to(column, (HB, N)) == node).astype(F32))
+    return jnp.concatenate(picked, axis=0).astype(BF)
+
+
 def greet(devices):
     barrier = pltpu.get_barrier_semaphore()
     for device in devices:
@@ -78,7 +101,7 @@
     n_dom,
     snd_ref, rcv_ref, rows_ref, h_hbm, e_hbm, pin_hbm, b_in,
     halo_ref, thalo_ref, pre_hbm,
-    h_v, x_v, pin_v, t_v, pre_v, wide, outgoing, incoming,
+    h_v, x_v, pin_v, t_v, pre_v, outgoing, incoming,
     in_sem, e_sem, pre_sem, send_sem, recv_sem,
 ):
     me = lax.axis_index("dom")
@@ -103,11 +126,7 @@
     for i in range(CHUNKS):
         e_load(i).start()
     h_load.wait()
-    wide[...] = h_v[...].astype(F32)
-    for s in range(SLOTS):
-        for k in range(HB):
-            row = rows_ref[k, targets[s]]
-            outgoing[pl.ds(s * HB + k, 1), :] = wide[pl.ds(row, 1), :]
+    outgoing[...] = mm(boundary_rows(rows_ref, targets), h_v[...])
     pl.semaphore_wait(barrier, SLOTS)
     copies = []
     for s in range(SLOTS):
@@ -152,13 +171,12 @@
 def run_halo(n_dom, *operands):
     hbm = pl.BlockSpec(memory_space=pl.ANY)
     vmem = pl.BlockSpec(memory_space=pltpu.VMEM)
-    smem = pl.BlockSpec(memory_space=pltpu.SMEM)
     shape = jax.ShapeDtypeStruct
     dma = pltpu.SemaphoreType.DMA
     return pl.pallas_call(
         functools.partial(halo_kernel, n_dom),
         out_shape=[shape((HPAD, L), BF), shape((HPAD, L), BF), shape((E, L), BF)],
-        in_specs=[vmem, vmem, smem, hbm, hbm, hbm, vmem],
+        in_specs=[vmem, vmem, vmem, hbm, hbm, hbm, vmem],
         out_specs=[vmem, vmem, hbm],
         scratch_shapes=[
             pltpu.VMEM((N, L), BF),
@@ -166,7 +184,6 @@
             pltpu.VMEM((3 * L, L), BF),
             pltpu.VMEM((3 * L, L), BF),
             pltpu.VMEM((E, L), BF),
-            pltpu.VMEM((N, L), F32),
             pltpu.VMEM((HALO, L), F32),
             pltpu.VMEM((HALO, L), F32),
             dma((2,)),
@@ -252,25 +269,32 @@
     high = lax.broadcasted_iota(I32, (N, 128), 0)
     loads[0].wait()
 
-    def forward(i, carry):
-        for b in range(C // 128):
-            block = i * (C // 128) + b
-            at = pl.ds(pl.multiple_of(block * 128, 128), 128)
+    def forward_rows(first):
+        for b in range(S // 128):
+            at = pl.ds(pl.multiple_of(first + b * 128, 128), 128)
+            block = first // 128 + b
             r_row = rcv_ref[pl.ds(block, 1), :]
             x_v[at, 0:HPAD] = one_hot_columns(idx_v[pl.ds(block, 1), :] - N, lane, 1)
             x_v[at, HPAD:] = one_hot_columns(r_row, lane, N // 128)
             rt_v[:, at] = (jnp.broadcast_to(r_row, (N, 128)) == high).astype(F32).astype(BF)
+        at = pl.ds(pl.multiple_of(first, S), S)
+        pre = part_v[at, :].astype(F32) + mm(x_v[at, 0:HPAD], thalo_ref[...])
+        yield
+        pre_v[at, :] = pre
+        hid = (pre * sigmoid(pre)).astype(BF)
+        hid_v[at, :] = hid
+        yield
+        raw = mm(hid, pout_v[...]) + b_out[...]
+        yield
+        normed, inv = norm_forward(raw)
+        n_v[at, :] = normed
+        inv_v[at, :] = inv
+        enew_v[at, :] = (e_v[at, :].astype(F32) + normed * gain[...]).astype(BF)
+
+    def forward(i, carry):
         part_load(i).wait()
-        pre = part_v[rows(i), :].astype(F32) + mm(x_v[rows(i), 0:HPAD], thalo_ref[...])
-        pre_v[rows(i), :] = pre
-        hid = (pre * sigmoid(pre)).astype(BF)
-        hid_v[rows(i), :] = hid
-        raw = mm(hid, pout_v[...]) + b_out[...]
-        normed, inv = norm_forward(raw)
-        n_v[rows(i), :] = normed
-        inv_v[rows(i), :] = inv
         e_load(i).wait()
-        enew_v[rows(i), :] = (e_v[rows(i), :].astype(F32) + normed * gain[...]).astype(BF)
+        staggered(*[forward_rows(i * C + s * S) for s in range(C // S)])
         put(i, enew_v, eout_hbm, eout_sem).start()
         put(i, hid_v, hid_hbm, hid_sem).start()
         return carry
@@ -303,16 +327,25 @@
     gnode_copy = pltpu.make_async_copy(gnode_v, gnode_hbm, out_sem.at[2])
     gnode_copy.start()
 
+    def backward_rows(first):
+        at = pl.ds(pl.multiple_of(first, S), S)
+        total = cot_v[at, :] + mm(x_v[at, HPAD:], dy_v[...])
+        yield
+        draw = norm_backward(total * gain[...], n_v[at, :], inv_v[at, :]).astype(BF)
+        draw_v[at, :] = draw
+        yield
+        dhid = mm_nt(draw, pout_v[...])
+        yield
+        dpre = (dhid * act_slope(pre_v[at, :])).astype(BF)
+        dpre_v[at, :] = dpre
+        yield
+        cot_v[at, :] = total + mm_nt(dpre, pe_v[...])
+
     def backward(i, carry):
         cot_load(i).wait()
-        total = cot_v[rows(i), :] + mm(x_v[rows(i), HPAD:], dy_v[...])
-        draw = norm_backward(total * gain[...], n_v[rows(i), :], inv_v[rows(i), :]).astype(BF)
-        draw_v[rows(i), :] = draw
+        staggered(*[backward_rows(i * C + s * S) for s in range(C // S)])
         put(i, draw_v, draw_hbm, draw_sem).start()
-        dpre = (mm_nt(draw, pout_v[...]) * act_slope(pre_v[rows(i), :])).astype(BF)
-        dpre_v[rows(i), :] = dpre
         put(i, dpre_v, dpre_hbm, dpre_sem).start()
-        cot_v[rows(i), :] = total + mm_nt(dpre, pe_v[...])
         put(i, cot_v, egrad_hbm, egrad_sem).start()
         return carry
 
@@ -488,9 +521,9 @@
 
 def sums_kernel(
     n_dom,
-    snd_ref, rcv_ref, gnode_hbm, h_hbm, halo_hbm, e_hbm, pin_hbm, hid_hbm, draw_hbm, dpre_hbm,
-    out_ref, part_ref, ret_ref,
-    tab_v, e_v, hid_v, draw_v, dpre_v, ps_v, pr_v, st_v, rt_v, as_v, ar_v, there_in, there_out, y_v,
+    snd_ref, rcv_ref, rows_ref, gnode_hbm, h_hbm, halo_hbm, e_hbm, pin_hbm, hid_hbm, draw_hbm, dpre_hbm,
+    out_ref, part_ref,
+    tab_v, e_v, hid_v, draw_v, dpre_v, ps_v, pr_v, st_v, rt_v, as_v, ar_v, there_in, there_out, y_v, ret_ref, part_v,
     block, sorted_v, got, in_sem, y_send, y_recv, last_send, last_recv,
     *wave_refs,
 ):
@@ -516,13 +549,13 @@
         copy.start()
         loads.append(copy)
 
-    load(dpre_hbm.at[:, theirs], dpre_v.at[0])
-    load(h_hbm, tab_v.at[pl.ds(0, N)])
-    load(halo_hbm, tab_v.at[pl.ds(N, HPAD)])
-    load(e_hbm, e_v)
     for lanes in range(2):
         for k in range(4):
             load(gnode_hbm.at[2 * c + lanes, pl.ds(4 * k, 4)], node_wave.own.at[lanes, k])
+    load(dpre_hbm.at[:, theirs], dpre_v.at[0])
+    load(e_hbm, e_v)
+    load(h_hbm, tab_v.at[pl.ds(0, N)])
+    load(halo_hbm, tab_v.at[pl.ds(N, HPAD)])
     load(dpre_hbm.at[:, mine], dpre_v.at[1])
     load(hid_hbm, hid_v)
     load(draw_hbm.at[:, theirs], draw_v.at[0])
@@ -567,13 +600,13 @@
     def out_products(half, dst):
         put_lanes(mm_tn(hid_v[...], draw_v[half]), dst, 32)
 
-    for k in range(4):
+    for k in range(8):
+        loads[k].wait()
+    node_wave.first()
+    for k in range(8, 12):
         loads[k].wait()
     in_products(0, there_in)
     in_wave.to_core(there_in)
-    for k in range(4, 12):
-        loads[k].wait()
-    node_wave.first()
     loads[12].wait()
     in_products(1, in_wave.own)
     in_wave.first()
@@ -599,14 +632,18 @@
         copy.start()
         returns.append(copy)
     in_wave.second()
-    part_ref[...] = (
+    part_v[...] = (
         mm_nt(as_v[0, 0:N, :], ps_v[0])
         + mm_nt(as_v[1, 0:N, :], ps_v[1])
         + mm_nt(ar_v[0], pr_v[0])
         + mm_nt(ar_v[1], pr_v[1])
-    ).astype(BF)
+    )
+    out_wave.second()
     node_wave.third(block, pl.ds(0, 96))
-    out_wave.second()
+    for copy in returns:
+        copy.wait()
+    readers = [lax.rem(me - slot_shift(s) + n_dom, n_dom) for s in range(SLOTS)]
+    part_ref[...] = (part_v[...] + mm_tn(boundary_rows(rows_ref, readers), ret_ref[...].astype(BF))).astype(BF)
     in_wave.third(block, pl.ds(96, 96))
     out_wave.third(block, pl.ds(192, 32))
 
@@ -649,8 +686,6 @@
     even = c == 0
     out_ref[:, 0:WIDE] = jnp.where(even, same, cross)
     out_ref[:, WIDE:] = jnp.where(even, cross, same)
-    for copy in returns:
-        copy.wait()
     for copy in lasts:
         copy.wait_send()
     for wave in (node_wave, in_wave, out_wave):
@@ -664,9 +699,9 @@
     dma = pltpu.SemaphoreType.DMA
     return pl.pallas_call(
         functools.partial(sums_kernel, n_dom),
-        out_shape=[shape((32, L), F32), shape((N, L), BF), shape((HALO, L), F32)],
-        in_specs=[vmem, vmem] + [hbm] * 8,
-        out_specs=[vmem, vmem, vmem],
+        out_shape=[shape((32, L), F32), shape((N, L), BF)],
+        in_specs=[vmem, vmem, vmem] + [hbm] * 8,
+        out_specs=[vmem, vmem],
         scratch_shapes=[
             pltpu.VMEM((TAB, L), BF),
             pltpu.VMEM((E, L), BF),
@@ -682,6 +717,8 @@
             pltpu.VMEM((2, 4, 4, 96, LANES), BF),
             pltpu.VMEM((2, 4, 4, 32, LANES), BF),
             pltpu.VMEM((HALO, L), F32),
+            pltpu.VMEM((HALO, L), F32),
+            pltpu.VMEM((N, L), F32),
             pltpu.VMEM((224, WIDE), BF),
             pltpu.VMEM((8, 32, WIDE), BF),
             pltpu.VMEM((7, 32, WIDE), BF),
@@ -702,29 +739,20 @@
 
 
 def last_kernel(
-    n_dom, edge_factor, node_factor,
-    rows_ref, sums_ref, part_ref, ret_ref, npart_ref,
-    grad_ref, ein_ref, eout_ref, nin_ref, nout_ref,
+    edge_factor, node_factor, sums_ref, part_ref, npart_ref, grad_ref, ein_ref, eout_ref, nin_ref, nout_ref
 ):
-    me = lax.axis_index("dom")
     grad_ref[...] = npart_ref[...] + part_ref[...].astype(F32)
-    for s in range(SLOTS):
-        reader = lax.rem(me - slot_shift(s) + n_dom, n_dom)
-        for k in range(HB):
-            at = pl.ds(rows_ref[k, reader], 1)
-            grad_ref[at, :] = grad_ref[at, :] + ret_ref[s * HB + k : s * HB + k + 1, :]
     nin_ref[0] = sums_ref[0:8, :] * node_factor
     nout_ref[0] = sums_ref[8:12, :] * node_factor
     ein_ref[...] = (sums_ref[12:24, :] * edge_factor).reshape(12, 1, L)
     eout_ref[0] = sums_ref[24:28, :] * edge_factor
 
 
-def run_last(n_dom, edge_factor, node_factor, *operands):
+def run_last(edge_factor, node_factor, *operands):
     vmem = pl.BlockSpec(memory_space=pltpu.VMEM)
-    smem = pl.BlockSpec(memory_space=pltpu.SMEM)
     shape = jax.ShapeDtypeStruct
     return pl.pallas_call(
-        functools.partial(last_kernel, n_dom, edge_factor, node_factor),
+        functools.partial(last_kernel, edge_factor, node_factor),
         out_shape=[
             shape((N, L), F32),
             shape((12, 1, L), F32),
@@ -732,7 +760,7 @@
             shape((1, 8, L), F32),
             shape((1, 4, L), F32),
         ],
-        in_specs=[smem, vmem, vmem, vmem, vmem],
+        in_specs=[vmem] * 3,
         out_specs=[vmem] * 5,
         name="last",
     )(*operands)
@@ -771,13 +799,13 @@
         edge_bias_out, edge_gain, node_proj_in.reshape(2 * L, L), node_bias_in,
         node_proj_out.reshape(L, L), node_bias_out, node_gain, node_cot, edge_cot,
     )
-    sums, part, returned = run_sums(
-        n_dom, snd, rcv, gnode, node_latent, halo, edge_latent, pin, hid, draw, dpre
+    sums, part = run_sums(
+        n_dom, snd, rcv, slot_rows, gnode, node_latent, halo, edge_latent, pin, hid, draw, dpre
     )
     edge_factor = float(E * n_dom) ** (-0.5)
     node_factor = float(N * n_dom) ** (-0.5)
     node_grad, edge_in, edge_out_grad, node_in, node_out_grad = run_last(
-        n_dom, edge_factor, node_factor, slot_rows, sums, part, returned, npart
+        edge_factor, node_factor, sums, part, npart
     )
     edge_in = edge_in.transpose(1, 0, 2)
     return node_out, edge_out, node_grad, edge_grad, edge_in, edge_out_grad, node_in, node_out_grad

time: 74.1 us -> 72 us (0.972)
  Pallas kernels: 72.5 us -> 70.3 us
    pallas_call x1, Pallas kernels: 31 us -> 29.7 us  [run_sums(): pl.pallas_call(functools.partial(sums_kernel, n_dom), out_shape=[shape((3...]
where the time goes in v3:
time: 72 us; the launch traced here: 71.6 us
  Pallas kernels  70.3 us (98%)
  between operations  1.3 us (2%)
    pallas_call x1, Pallas kernels, run_sums(): pl.pallas_call(functools.partial(sums_kernel, n_dom), out_shape=[shape((3...  29.7 us
    pallas_call x1, Pallas kernels, run_rows(): pl.pallas_call(functools.partial(rows_kernel, n_dom), out_shape=[shape((N...  20.1 us
    pallas_call x1, Pallas kernels, run_halo(): pl.pallas_call(functools.partial(halo_kernel, n_dom), out_shape=[shape((H...  18 us
    pallas_call x1, Pallas kernels, run_last(): pl.pallas_call(functools.partial(last_kernel, edge_factor, node_factor),...  2.48 us

profile of v3, /device:TPU:1, one launch (start us, length us, event | category | flops | bytes accessed | tf_op | source)
XLA Modules:
  0.0 71.6 jit_solution(2802162744497621426)
XLA Ops:
  1.3 18.0 %halo.1 = (bf16[128,512]{1,0:T(8,128)(2,1)}, bf16[128,512]{1,0:T(8,128)(2,1)}, bf16[2048,512]{1,0:T(8,128)(2,1)}) custom-call(s32[16,128]{1,0:T(8,128)} %bitcast.16, s32[16,128]{1,0:T(8,128)} %bitcast.19, s32[8,128]{1,0:T(8,128)} %bitcast.22, bf16[512,512]{1,0:T(8,128)(2,1)} %h_hbm.5, bf16[2048,512]{1,0:T(8,128)(2,1)} %e_hbm.5, bf16[1536,512]{1,0:T(8,128)(2,1)} %bitcast.10, ...), custom_call_target="tpu_custom_call" | custom-call | tf_op jit(solution)/shard_map/halo/pallas_call | solution.py:176
  19.3 20.1 %rows.1 = (bf16[512,512]{1,0:T(8,128)(2,1)}, bf16[2048,512]{1,0:T(8,128)(2,1)}, f32[2048,512]{1,0:T(8,128)}, bf16[2048,512]{1,0:T(8,128)(2,1)}, bf16[2048,512]{1...) custom-call(s32[16,128]{1,0:T(8,128)} %bitcast.17, ...), custom_call_target="tpu_custom_call" | custom-call | tf_op jit(solution)/shard_map/rows/pallas_call | solution.py:370
  39.4 29.7 %sums.1 = (f32[32,512]{1,0:T(8,128)}, bf16[512,512]{1,0:T(8,128)(2,1)}) custom-call(s32[16,128]{1,0:T(8,128)} %bitcast.18, s32[16,128]{1,0:T(8,128)} %bitcast.21, s32[8,128]{1,0:T(8,128)} %bitcast.23, bf16[4,16,96,128]{3,2,1,0:T(8,128)(2,1)} %get-tuple-element.30.gnode_hbm, bf16[512,512]{1,0:T(8,128)(2,1)} %h_hbm.5, ...), custom_call_target="tpu_custom_call" | custom-call | tf_op jit(solution)/shard_map/sums/pallas_call | solution.py:700
  69.1 2.5 %last.1 = (f32[512,512]{1,0:T(8,128)}, f32[12,1,512]{2,1,0:T(1,128)}, f32[1,4,512]{2,1,0:T(4,128)}, f32[1,8,512]{2,1,0:T(8,128)}, f32[1,4,512]{2,1,0:T(4,128)}) custom-call(f32[32,512]{1,0:T(8,128)} %get-tuple-element.35.sums_ref, bf16[512,512]{1,0:T(8,128)(2,1)} %get-tuple-element.36.part_ref, f32[512,512]{1,0:T(8,128)} %get-tuple-element.37.npart_ref), custom_call_target="tpu_custom_call" | custom-call | tf_op jit(solution)/shard_map/last/pallas_call | solution.py:754

commit v4 on v3

--- a/solution.py
+++ b/solution.py
@@ -147,18 +147,21 @@
     t_v[2 * L :, :] = (mm(h_v[...], pin_v[2 * L :, :]) + b_in[...]).astype(BF)
     lane = lax.broadcasted_iota(I32, (128, 128), 1)
 
-    def local(i, carry):
-        for b in range(C // 128):
-            block = i * (C // 128) + b
-            at = pl.ds(pl.multiple_of(block * 128, 128), 128)
-            x_v[at, L : 2 * L] = one_hot_columns(snd_ref[pl.ds(block, 1), :], lane, N // 128)
-            x_v[at, 2 * L :] = one_hot_columns(rcv_ref[pl.ds(block, 1), :], lane, N // 128)
-        e_load(i).wait()
-        pre_v[rows(i), :] = mm(x_v[rows(i), :], t_v[...]).astype(BF)
-        pre_put(i).start()
-        return carry
-
-    lax.fori_loop(0, CHUNKS, local, 0)
+    def local(first):
+        if first % C == 0:
+            e_load(first // C).wait()
+        for b in range(S // 128):
+            at = pl.ds(first + b * 128, 128)
+            block = pl.ds(first // 128 + b, 1)
+            x_v[at, L : 2 * L] = one_hot_columns(snd_ref[block, :], lane, N // 128)
+            x_v[at, 2 * L :] = one_hot_columns(rcv_ref[block, :], lane, N // 128)
+        yield
+        at = pl.ds(first, S)
+        pre_v[at, :] = mm(x_v[at, :], t_v[...]).astype(BF)
+        if (first + S) % C == 0:
+            pre_put(first // C).start()
+
+    staggered(*[local(s * S) for s in range(E // S)])
     for copy in copies:
         copy.wait()
     halo = jnp.concatenate([incoming[...].astype(BF), jnp.zeros((HPAD - HALO, L), BF)], axis=0)
@@ -222,7 +225,7 @@
     npin_hbm, nb_in, npout_hbm, nb_out, ngain, ncot_hbm, ecot_hbm,
     nout_hbm, eout_hbm, egrad_hbm, dpre_hbm, draw_hbm, hid_hbm, gnode_hbm, npart_hbm,
     idx_v, x_v, rt_v, e_v, part_v, h_v, pe_v, pout_v, npin_v, npout_v, ncot_v, cot_v,
-    pre_v, hid_v, n_v, inv_v, enew_v, draw_v, dpre_v, nx_v, dy_v, nout_v, npart_v, gnode_v,
+    slope_v, hid_v, n_v, inv_v, enew_v, draw_v, dpre_v, nx_v, dy_v, nout_v, npart_v, gnode_v,
     in_sem, e_sem, part_sem, cot_sem, eout_sem, hid_sem, draw_sem, dpre_sem, egrad_sem, out_sem,
 ):
     me = lax.axis_index("dom")
@@ -270,6 +273,9 @@
     loads[0].wait()
 
     def forward_rows(first):
+        if first % C == 0:
+            part_load(first // C).wait()
+            e_load(first // C).wait()
         for b in range(S // 128):
             at = pl.ds(pl.multiple_of(first + b * 128, 128), 128)
             block = first // 128 + b
@@ -280,8 +286,10 @@
         at = pl.ds(pl.multiple_of(first, S), S)
         pre = part_v[at, :].astype(F32) + mm(x_v[at, 0:HPAD], thalo_ref[...])
         yield
-        pre_v[at, :] = pre
-        hid = (pre * sigmoid(pre)).astype(BF)
+        gate = sigmoid(pre)
+        hidden = pre * gate
+        slope_v[at, :] = (gate + hidden * (1.0 - gate)).astype(BF)
+        hid = hidden.astype(BF)
         hid_v[at, :] = hid
         yield
         raw = mm(hid, pout_v[...]) + b_out[...]
@@ -290,16 +298,11 @@
         n_v[at, :] = normed
         inv_v[at, :] = inv
         enew_v[at, :] = (e_v[at, :].astype(F32) + normed * gain[...]).astype(BF)
-
-    def forward(i, carry):
-        part_load(i).wait()
-        e_load(i).wait()
-        staggered(*[forward_rows(i * C + s * S) for s in range(C // S)])
-        put(i, enew_v, eout_hbm, eout_sem).start()
-        put(i, hid_v, hid_hbm, hid_sem).start()
-        return carry
-
-    lax.fori_loop(0, CHUNKS, forward, 0)
+        if (first + S) % C == 0:
+            put(first // C, enew_v, eout_hbm, eout_sem).start()
+            put(first // C, hid_v, hid_hbm, hid_sem).start()
+
+    staggered(*[forward_rows(s * S) for s in range(E // S)])
 
     valid = (lax.broadcasted_iota(I32, (N, 1), 0) < cnt_ref[0]).astype(F32)
     nx_v[:, L:] = (mm(rt_v[...], enew_v[...]) * valid).astype(BF)
@@ -328,6 +331,8 @@
     gnode_copy.start()
 
     def backward_rows(first):
+        if first % C == 0:
+            cot_load(first // C).wait()
         at = pl.ds(pl.multiple_of(first, S), S)
         total = cot_v[at, :] + mm(x_v[at, HPAD:], dy_v[...])
         yield
@@ -336,20 +341,16 @@
         yield
         dhid = mm_nt(draw, pout_v[...])
         yield
-        dpre = (dhid * act_slope(pre_v[at, :])).astype(BF)
+        dpre = (dhid * slope_v[at, :].astype(F32)).astype(BF)
         dpre_v[at, :] = dpre
         yield
         cot_v[at, :] = total + mm_nt(dpre, pe_v[...])
-
-    def backward(i, carry):
-        cot_load(i).wait()
-        staggered(*[backward_rows(i * C + s * S) for s in range(C // S)])
-        put(i, draw_v, draw_hbm, draw_sem).start()
-        put(i, dpre_v, dpre_hbm, dpre_sem).start()
-        put(i, cot_v, egrad_hbm, egrad_sem).start()
-        return carry
-
-    lax.fori_loop(0, CHUNKS, backward, 0)
+        if (first + S) % C == 0:
+            put(first // C, draw_v, draw_hbm, draw_sem).start()
+            put(first // C, dpre_v, dpre_hbm, dpre_sem).start()
+            put(first // C, cot_v, egrad_hbm, egrad_sem).start()
+
+    staggered(*[backward_rows(s * S) for s in range(E // S)])
     nout_copy.wait()
     npart_copy.wait()
     gnode_copy.wait()
@@ -395,7 +396,7 @@
             pltpu.VMEM((L, L), BF),
             pltpu.VMEM((N, L), F32),
             pltpu.VMEM((E, L), F32),
-            pltpu.VMEM((E, L), F32),
+            pltpu.VMEM((E, L), BF),
             pltpu.VMEM((E, L), BF),
             pltpu.VMEM((E, L), F32),
             pltpu.VMEM((E, 1), F32),
@@ -632,21 +633,14 @@
         copy.start()
         returns.append(copy)
     in_wave.second()
+    out_wave.second()
     part_v[...] = (
         mm_nt(as_v[0, 0:N, :], ps_v[0])
         + mm_nt(as_v[1, 0:N, :], ps_v[1])
         + mm_nt(ar_v[0], pr_v[0])
         + mm_nt(ar_v[1], pr_v[1])
     )
-    out_wave.second()
     node_wave.third(block, pl.ds(0, 96))
-    for copy in returns:
-        copy.wait()
-    readers = [lax.rem(me - slot_shift(s) + n_dom, n_dom) for s in range(SLOTS)]
-    part_ref[...] = (part_v[...] + mm_tn(boundary_rows(rows_ref, readers), ret_ref[...].astype(BF))).astype(BF)
-    in_wave.third(block, pl.ds(96, 96))
-    out_wave.third(block, pl.ds(192, 32))
-
     row = lax.broadcasted_iota(I32, (256, 224), 0)
     col = lax.broadcasted_iota(I32, (256, 224), 1)
     j = row // 32
@@ -661,6 +655,13 @@
         ),
     )
     order = (source == col).astype(F32).astype(BF)
+    for copy in returns:
+        copy.wait()
+    readers = [lax.rem(me - slot_shift(s) + n_dom, n_dom) for s in range(SLOTS)]
+    part_ref[...] = (part_v[...] + mm_tn(boundary_rows(rows_ref, readers), ret_ref[...].astype(BF))).astype(BF)
+    in_wave.third(block, pl.ds(96, 96))
+    out_wave.third(block, pl.ds(192, 32))
+
     sorted_v[...] = mm(order, block[...]).astype(BF).reshape(8, 32, WIDE)
     lasts = []
     for o in range(1, 8):

time: 72 us -> 70.1 us (0.974)
  Pallas kernels: 70.3 us -> 68.2 us
    pallas_call x1, Pallas kernels: 20.1 us -> 18.4 us  [run_rows(): pl.pallas_call(functools.partial(rows_kernel, n_dom), out_shape=[shape((N...]
    pallas_call x1, Pallas kernels: 18 us -> 17.1 us  [run_halo(): pl.pallas_call(functools.partial(halo_kernel, n_dom), out_shape=[shape((H...]
where the time goes in v4:
time: 70.1 us; the launch traced here: 69.5 us
  Pallas kernels  68.2 us (97%)
  between operations  1.3 us (2%)
    pallas_call x1, Pallas kernels, run_sums(): pl.pallas_call(functools.partial(sums_kernel, n_dom), out_shape=[shape((3...  30.2 us
    pallas_call x1, Pallas kernels, run_rows(): pl.pallas_call(functools.partial(rows_kernel, n_dom), out_shape=[shape((N...  18.4 us
    pallas_call x1, Pallas kernels, run_halo(): pl.pallas_call(functools.partial(halo_kernel, n_dom), out_shape=[shape((H...  17.1 us
    pallas_call x1, Pallas kernels, run_last(): pl.pallas_call(functools.partial(last_kernel, edge_factor, node_factor),...  2.48 us

profile of v4, /device:TPU:1, one launch (start us, length us, event | category | flops | bytes accessed | tf_op | source)
XLA Modules:
  0.0 69.5 jit_solution(5644739771740530593)
XLA Ops:
  1.3 17.1 %halo.1 = (bf16[128,512]{1,0:T(8,128)(2,1)}, bf16[128,512]{1,0:T(8,128)(2,1)}, bf16[2048,512]{1,0:T(8,128)(2,1)}) custom-call(s32[16,128]{1,0:T(8,128)} %bitcast.16, s32[16,128]{1,0:T(8,128)} %bitcast.19, s32[8,128]{1,0:T(8,128)} %bitcast.22, bf16[512,512]{1,0:T(8,128)(2,1)} %h_hbm.5, bf16[2048,512]{1,0:T(8,128)(2,1)} %e_hbm.5, bf16[1536,512]{1,0:T(8,128)(2,1)} %bitcast.10, ...), custom_call_target="tpu_custom_call" | custom-call | tf_op jit(solution)/shard_map/halo/pallas_call | solution.py:179
  18.4 18.4 %rows.1 = (bf16[512,512]{1,0:T(8,128)(2,1)}, bf16[2048,512]{1,0:T(8,128)(2,1)}, f32[2048,512]{1,0:T(8,128)}, bf16[2048,512]{1,0:T(8,128)(2,1)}, bf16[2048,512]{1...) custom-call(s32[16,128]{1,0:T(8,128)} %bitcast.17, ...), custom_call_target="tpu_custom_call" | custom-call | tf_op jit(solution)/shard_map/rows/pallas_call | solution.py:371
  36.8 30.2 %sums.1 = (f32[32,512]{1,0:T(8,128)}, bf16[512,512]{1,0:T(8,128)(2,1)}) custom-call(s32[16,128]{1,0:T(8,128)} %bitcast.18, s32[16,128]{1,0:T(8,128)} %bitcast.21, s32[8,128]{1,0:T(8,128)} %bitcast.23, bf16[4,16,96,128]{3,2,1,0:T(8,128)(2,1)} %get-tuple-element.30.gnode_hbm, bf16[512,512]{1,0:T(8,128)(2,1)} %h_hbm.5, ...), custom_call_target="tpu_custom_call" | custom-call | tf_op jit(solution)/shard_map/sums/pallas_call | solution.py:701
  67.0 2.5 %last.1 = (f32[512,512]{1,0:T(8,128)}, f32[12,1,512]{2,1,0:T(1,128)}, f32[1,4,512]{2,1,0:T(4,128)}, f32[1,8,512]{2,1,0:T(8,128)}, f32[1,4,512]{2,1,0:T(4,128)}) custom-call(f32[32,512]{1,0:T(8,128)} %get-tuple-element.35.sums_ref, bf16[512,512]{1,0:T(8,128)(2,1)} %get-tuple-element.36.part_ref, f32[512,512]{1,0:T(8,128)} %get-tuple-element.37.npart_ref), custom_call_target="tpu_custom_call" | custom-call | tf_op jit(solution)/shard_map/last/pallas_call | solution.py:755
